TPU v7x, 1024 devices: a whole 8x8x8 slice. The times are simulated.
1024 devices in a mesh: row: 32 (over z, y_lo, core), col: 32 (over x, y_hi).
Axes of the slice: x: 8, y: 8 (y_hi: 4, y_lo: 2; y = y_hi * 2 + y_lo), z: 8, core: 2. Of those that a mesh axis runs over, the one named last changes fastest.
Arguments:
- left_blocks: bfloat16 [32, 576, 128, 128], P('row', 'col')
- left_slots: int32 [32, 576], P('row', 'col'), may hold values from 0 to 36, as said below
- right_blocks: bfloat16 [32, 576, 128, 128], P('row', 'col')
- right_slots: int32 [32, 576], P('row', 'col'), may hold values from 0 to 36, as said below
Outputs:
- product_window: bfloat16 [24576, 24576], P('row', 'col')
- trace_scaled: float32 [], replicated
- norm_scaled: float32 [], replicated
Inputs may be any that keep to these rules, and one draw needn't show every extreme that they name: `left_slots`: in each tile the live entries come first, are distinct and lie below 36; the others equal 36 and mark empty slots. Every tile has one live slot or more, and in every draw some tile has all 18 slots live. `right_slots`: as for left_slots.
All inputs are finite; a program needn't handle non-finite values.
Results may differ from a plain program's by a relative error of at most 0.001.
Values may be sent and summed in bfloat16 or wider, within the bound.
No kernel may reach another device: no remote copies, remote signals or barrier semaphores. Data moves between devices by JAX's collectives and lax.ppermute only.
A program may use at most 32 MiB of HBM per device.

v0:
```python
import math

import jax
import jax.numpy as jnp
from jax import lax
from jax.sharding import PartitionSpec as P

BLK = 128
TB = 6
STEPS = 4


def shifted(value, axis, steps):
    count = lax.axis_size(axis)
    pairs = [(source, (source + steps) % count) for source in range(count)]
    return lax.ppermute(value, axis, pairs)


def densify(blocks, positions):
    cell_count = TB * TB
    onehot = (jnp.arange(cell_count, dtype=jnp.int32)[:, None] == positions[None, :]).astype(
        jnp.bfloat16
    )
    placed = jnp.einsum("ps,sab->pab", onehot, blocks, preferred_element_type=jnp.float32).astype(
        jnp.bfloat16
    )
    return placed.reshape(TB, TB, BLK, BLK).transpose(0, 2, 1, 3).reshape(TB * BLK, TB * BLK)


def multiply(left_pair, right_pair):
    left_matrix = densify(left_pair[0], left_pair[1])
    right_matrix = densify(right_pair[0], right_pair[1])
    return jnp.dot(left_matrix, right_matrix, preferred_element_type=jnp.float32)


def body(left_blocks, left_slots, right_blocks, right_slots):
    left_block = left_blocks[0]
    left_cell = left_slots[0]
    right_block = right_blocks[0]
    right_cell = right_slots[0]
    running = multiply((left_block, left_cell), (right_block, right_cell))
    left_now = (left_block, left_cell)
    right_now = (right_block, right_cell)
    for step in range(1, STEPS):
        left_now = shifted((left_now[0], left_now[1]), "col", -1)
        right_now = shifted((right_now[0], right_now[1]), "row", -1)
        running = running + multiply(left_now, right_now)
    trace_part = jnp.trace(running)
    diagonal_sum = jnp.where(
        lax.axis_index("row") == lax.axis_index("col"), trace_part, jnp.zeros_like(trace_part)
    )
    square_sum = jnp.sum(running * running)
    totals = lax.psum((diagonal_sum, square_sum), ("row", "col"))
    tile_width = TB * BLK
    trace_scaled = totals[0] / math.sqrt(
        min(lax.axis_size("row"), lax.axis_size("col")) * tile_width
    )
    norm_scaled = totals[1] / (
        lax.axis_size("row") * lax.axis_size("col") * tile_width * tile_width
    )
    return (running.astype(jnp.bfloat16), trace_scaled, norm_scaled)


def solution(mesh):
    placed = (
        P("row", "col", None, None),
        P("row", "col"),
        P("row", "col", None, None),
        P("row", "col"),
    )
    return jax.shard_map(
        body, mesh=mesh, in_specs=placed, out_specs=(P("row", "col"), P(), P()), check_vma=False
    )
```

profile of v0, /device:TPU:1, one launch (start us, length us, event | category | flops | bytes accessed | tf_op | source)
XLA Modules:
  0.0 264.9 jit_solution(6945018641425171688)
XLA Ops:
  0.6 9.7 %collective-permute-start.1 = (bf16[18,128,128]{2,1,0:T(8,128)(2,1)}, bf16[18,128,128]{2,1,0:T(8,128)(2,1)}, u32[]{:S(2)}, u32[]{:S(2)}) collective-permute-start(bf16[18,128,128]{2,1,0:T(8,128)(2,1)} %bitcast.112), channel_id=1, source_target_pairs={{0,31},{1,0},{2,1},{3,2},{4,3},{5,4},{6,5},{7,6},{8,7},{9,8},{10,9... | collective-permute-start | bytes 1769480 | tf_op jit(solution)/shard_map/ppermute | solution.py:16
  10.3 3.5 %collective-permute-start = (s32[18]{0:T(128)}, s32[18]{0:T(128)S(1)}, u32[]{:S(2)}, u32[]{:S(2)}) collective-permute-start(s32[18]{0:T(128)} %bitcast.116), channel_id=1, source_target_pairs={{0,31},{1,0},{2,1},{3,2},{4,3},{5,4},{6,5},{7,6},{8,7},{9,8},{10,9... | collective-permute-start | bytes 224 | tf_op jit(solution)/shard_map/ppermute | solution.py:16
  13.9 6.7 %collective-permute-start.3 = (bf16[18,128,128]{2,1,0:T(8,128)(2,1)}, bf16[18,128,128]{2,1,0:T(8,128)(2,1)S(1)}, u32[]{:S(2)}, u32[]{:S(2)}) collective-permute-start(bf16[18,128,128]{2,1,0:T(8,128)(2,1)} %bitcast.114), channel_id=1, source_target_pairs={{0,992},{32,0},{64,32},{96,64},{128,96},{160,128},{192,160},{224,1... | collective-permute-start | bytes 1769480 | tf_op jit(solution)/shard_map/ppermute | solution.py:16
  20.6 14.3 %collective-permute-start.2 = (s32[18]{0:T(128)}, s32[18]{0:T(128)S(1)}, u32[]{:S(2)}, u32[]{:S(2)}) collective-permute-start(s32[18]{0:T(128)} %bitcast.118), channel_id=1, source_target_pairs={{0,992},{32,0},{64,32},{96,64},{128,96},{160,128},{192,160},{224,1... | collective-permute-start | bytes 224 | tf_op jit(solution)/shard_map/ppermute | solution.py:16
  34.9 1.8 convolution_convert_fusion.7
  37.0 2.0 copy.29
  39.9 2.0 copy.32
  41.9 3.0 %fusion.14 = f32[768,768]{1,0:T(8,128)S(1)} fusion(bf16[96,8,6,128]{3,2,1,0:T(8,128)(2,1)} %bitcast.109, bf16[96,8,6,128]{3,2,1,0:T(8,128)(2,1)} %bitcast.108), kind=kOutput, calls=%fused_computation.26 | convolution fusion | flops 905969664 | bytes 4718592 | tf_op jit(solution)/shard_map/dot_general | solution.py:33
  44.9 1.9 collective-permute-start.4
  46.8 3.1 %collective-permute-start.6 = (s32[18]{0:T(128)S(1)}, s32[18]{0:T(128)S(1)}, u32[]{:S(2)}, u32[]{:S(2)}) collective-permute-start(s32[18]{0:T(128)S(1)} %collective-permute-done.2), channel_id=1, source_target_pairs={{0,992},{32,0},{64,32},{96,64},{128,96},{160,128},{192,160},{224,1... | collective-permute-start | bytes 224 | tf_op jit(solution)/shard_map/ppermute | solution.py:16
  50.1 5.2 %collective-permute-start.8 = (s32[18]{0:T(128)S(1)}, s32[18]{0:T(128)S(1)}, u32[]{:S(2)}, u32[]{:S(2)}) collective-permute-start(s32[18]{0:T(128)S(1)} %collective-permute-done.4), channel_id=1, source_target_pairs={{0,31},{1,0},{2,1},{3,2},{4,3},{5,4},{6,5},{7,6},{8,7},{9,8},{10,9... | collective-permute-start | bytes 224 | tf_op jit(solution)/shard_map/ppermute | solution.py:16
  55.3 11.1 %collective-permute-start.10 = (s32[18]{0:T(128)S(1)}, s32[18]{0:T(128)S(1)}, u32[]{:S(2)}, u32[]{:S(2)}) collective-permute-start(s32[18]{0:T(128)S(1)} %collective-permute-done.6), channel_id=1, source_target_pairs={{0,992},{32,0},{64,32},{96,64},{128,96},{160,128},{192,160},{224,1... | collective-permute-start | bytes 224 | tf_op jit(solution)/shard_map/ppermute | solution.py:16
  66.5 1.8 convolution_convert_fusion.5
  68.5 0.8 copy.35
  69.3 1.9 collective-permute-start.5
  72.2 0.8 copy.38
  73.1 6.5 %collective-permute-start.7 = (bf16[18,128,128]{2,1,0:T(8,128)(2,1)S(1)}, bf16[18,128,128]{2,1,0:T(8,128)(2,1)S(1)}, u32[]{:S(2)}, u32[]{:S(2)}) collective-permute-start(bf16[18,128,128]{2,1,0:T(8,128)(2,1)S(1)} %collective-permute-done.3), channel_id=1, source_target_pairs={{0,992},{32,0},{64,32},{96,64},{128,96},{160,128},{192,160},{224,1... | collective-permute-start | bytes 1769480 | tf_op jit(solution)/shard_map/ppermute | solution.py:16
  79.6 1.1 fusion.9
  80.7 14.6 %collective-permute-done.5 = bf16[18,128,128]{2,1,0:T(8,128)(2,1)S(1)} collective-permute-done((bf16[18,128,128]{2,1,0:T(8,128)(2,1)}, bf16[18,128,128]{2,1,0:T(8,128)(2,1)S(1)}, u32[]{:S(2)}, u32[]{:S(2)}) %collective-permute-start.5) | collective-permute-done | bytes 589856 | tf_op jit(solution)/shard_map/ppermute | solution.py:16
  95.3 0.7 convolution_convert_fusion.3
  96.3 0.8 copy.41
  97.1 2.1 collective-permute-start.9
  99.2 28.3 %collective-permute-done.7 = bf16[18,128,128]{2,1,0:T(8,128)(2,1)S(1)} collective-permute-done((bf16[18,128,128]{2,1,0:T(8,128)(2,1)S(1)}, bf16[18,128,128]{2,1,0:T(8,128)(2,1)S(1)}, u32[]{:S(2)}, u32[]{:S(2)}) %collective-permute-start.7) | collective-permute-done | bytes 589856 | tf_op jit(solution)/shard_map/ppermute | solution.py:16
  127.6 0.7 convolution_convert_fusion.2
  128.6 0.8 copy.44
  129.4 1.9 collective-permute-start.11
  131.3 1.1 fusion.4
  133.4 0.8 copy.47
  134.3 6.3 %collective-permute-done.11 = bf16[18,128,128]{2,1,0:T(8,128)(2,1)S(1)} collective-permute-done((bf16[18,128,128]{2,1,0:T(8,128)(2,1)S(1)}, bf16[18,128,128]{2,1,0:T(8,128)(2,1)S(1)}, u32[]{:S(2)}, u32[]{:S(2)}) %collective-permute-start.11) | collective-permute-done | bytes 589856 | tf_op jit(solution)/shard_map/ppermute | solution.py:16
  141.6 0.8 copy.50
  142.4 2.8 %multiply_reduce_fusion = (f32[]{:T(128)}, f32[]{:T(128)}, bf16[768,768]{1,0:T(8,128)(2,1)}) fusion(bf16[96,8,6,128]{3,2,1,0:T(8,128)(2,1)S(1)} %bitcast.97, bf16[96,8,6,128]{3,2,1,0:T(8,128)(2,1)S(1)} %bitcast.96, f32[768,768]{1,0:T(8,128)S(1)} %fusion.4, f32[768,768]{1,0:T(8,128)S(1)} %fusion.14, f32[768,768]{1,0:T(8,128)S(1)} %fusion.9), kind=kOutput, calls=%fused_computation | convolution fusion | flops 911278080 | bytes 10616840 | tf_op jit(solution)/shard_map/dot_general | solution.py:33
  145.9 115.4 %all-reduce = (f32[]{:T(128)}, f32[]{:T(128)}) all-reduce(f32[]{:T(128)S(6)} %select_n.10, f32[]{:T(128)} %get-tuple-element.3), channel_id=1, replica_groups=mesh['row'=32,'col'=32] {'row','col'}, use_global_device_ids=true, to_apply=%region_1.2 | all-reduce | flops 2 | bytes 16 | tf_op jit(solution)/shard_map/psum | solution.py:53
  (25 shorter events, 5.1 us)
Async XLA Ops:
  0.6 65.8 %collective-permute-start.1 = (bf16[18,128,128]{2,1,0:T(8,128)(2,1)}, bf16[18,128,128]{2,1,0:T(8,128)(2,1)}, u32[]{:S(2)}, u32[]{:S(2)}) collective-permute-start(bf16[18,128,128]{2,1,0:T(8,128)(2,1)} %bitcast.112), channel_id=1, source_target_pairs={{0,31},{1,0},{2,1},{3,2},{4,3},{5,4},{6,5},{7,6},{8,7},{9,8},{10,9... | collective-permute-start | bytes 1769480 | tf_op jit(solution)/shard_map/ppermute | solution.py:16
  10.3 34.5 %collective-permute-start = (s32[18]{0:T(128)}, s32[18]{0:T(128)S(1)}, u32[]{:S(2)}, u32[]{:S(2)}) collective-permute-start(s32[18]{0:T(128)} %bitcast.116), channel_id=1, source_target_pairs={{0,31},{1,0},{2,1},{3,2},{4,3},{5,4},{6,5},{7,6},{8,7},{9,8},{10,9... | collective-permute-start | bytes 224 | tf_op jit(solution)/shard_map/ppermute | solution.py:16
  13.9 57.4 %collective-permute-start.3 = (bf16[18,128,128]{2,1,0:T(8,128)(2,1)}, bf16[18,128,128]{2,1,0:T(8,128)(2,1)S(1)}, u32[]{:S(2)}, u32[]{:S(2)}) collective-permute-start(bf16[18,128,128]{2,1,0:T(8,128)(2,1)} %bitcast.114), channel_id=1, source_target_pairs={{0,992},{32,0},{64,32},{96,64},{128,96},{160,128},{192,160},{224,1... | collective-permute-start | bytes 1769480 | tf_op jit(solution)/shard_map/ppermute | solution.py:16
  20.6 26.3 %collective-permute-start.2 = (s32[18]{0:T(128)}, s32[18]{0:T(128)S(1)}, u32[]{:S(2)}, u32[]{:S(2)}) collective-permute-start(s32[18]{0:T(128)} %bitcast.118), channel_id=1, source_target_pairs={{0,992},{32,0},{64,32},{96,64},{128,96},{160,128},{192,160},{224,1... | collective-permute-start | bytes 224 | tf_op jit(solution)/shard_map/ppermute | solution.py:16
  37.0 2.0 copy-start
  37.0 2.0 copy-start.1
  44.9 5.2 %collective-permute-start.4 = (s32[18]{0:T(128)S(1)}, s32[18]{0:T(128)S(1)}, u32[]{:S(2)}, u32[]{:S(2)}) collective-permute-start(s32[18]{0:T(128)S(1)} %collective-permute-done), channel_id=1, source_target_pairs={{0,31},{1,0},{2,1},{3,2},{4,3},{5,4},{6,5},{7,6},{8,7},{9,8},{10,9... | collective-permute-start | bytes 224 | tf_op jit(solution)/shard_map/ppermute | solution.py:16
  46.8 8.5 %collective-permute-start.6 = (s32[18]{0:T(128)S(1)}, s32[18]{0:T(128)S(1)}, u32[]{:S(2)}, u32[]{:S(2)}) collective-permute-start(s32[18]{0:T(128)S(1)} %collective-permute-done.2), channel_id=1, source_target_pairs={{0,992},{32,0},{64,32},{96,64},{128,96},{160,128},{192,160},{224,1... | collective-permute-start | bytes 224 | tf_op jit(solution)/shard_map/ppermute | solution.py:16
  50.1 82.3 %collective-permute-start.8 = (s32[18]{0:T(128)S(1)}, s32[18]{0:T(128)S(1)}, u32[]{:S(2)}, u32[]{:S(2)}) collective-permute-start(s32[18]{0:T(128)S(1)} %collective-permute-done.4), channel_id=1, source_target_pairs={{0,31},{1,0},{2,1},{3,2},{4,3},{5,4},{6,5},{7,6},{8,7},{9,8},{10,9... | collective-permute-start | bytes 224 | tf_op jit(solution)/shard_map/ppermute | solution.py:16
  55.3 78.9 %collective-permute-start.10 = (s32[18]{0:T(128)S(1)}, s32[18]{0:T(128)S(1)}, u32[]{:S(2)}, u32[]{:S(2)}) collective-permute-start(s32[18]{0:T(128)S(1)} %collective-permute-done.6), channel_id=1, source_target_pairs={{0,992},{32,0},{64,32},{96,64},{128,96},{160,128},{192,160},{224,1... | collective-permute-start | bytes 224 | tf_op jit(solution)/shard_map/ppermute | solution.py:16
  69.3 26.0 %collective-permute-start.5 = (bf16[18,128,128]{2,1,0:T(8,128)(2,1)}, bf16[18,128,128]{2,1,0:T(8,128)(2,1)S(1)}, u32[]{:S(2)}, u32[]{:S(2)}) collective-permute-start(bf16[18,128,128]{2,1,0:T(8,128)(2,1)} %collective-permute-done.1), channel_id=1, source_target_pairs={{0,31},{1,0},{2,1},{3,2},{4,3},{5,4},{6,5},{7,6},{8,7},{9,8},{10,9... | collective-permute-start | bytes 1769480 | tf_op jit(solution)/shard_map/ppermute | solution.py:16
  73.1 54.5 %collective-permute-start.7 = (bf16[18,128,128]{2,1,0:T(8,128)(2,1)S(1)}, bf16[18,128,128]{2,1,0:T(8,128)(2,1)S(1)}, u32[]{:S(2)}, u32[]{:S(2)}) collective-permute-start(bf16[18,128,128]{2,1,0:T(8,128)(2,1)S(1)} %collective-permute-done.3), channel_id=1, source_target_pairs={{0,992},{32,0},{64,32},{96,64},{128,96},{160,128},{192,160},{224,1... | collective-permute-start | bytes 1769480 | tf_op jit(solution)/shard_map/ppermute | solution.py:16
  97.1 35.3 %collective-permute-start.9 = (bf16[18,128,128]{2,1,0:T(8,128)(2,1)S(1)}, bf16[18,128,128]{2,1,0:T(8,128)(2,1)S(1)}, u32[]{:S(2)}, u32[]{:S(2)}) collective-permute-start(bf16[18,128,128]{2,1,0:T(8,128)(2,1)S(1)} %collective-permute-done.5), channel_id=1, source_target_pairs={{0,31},{1,0},{2,1},{3,2},{4,3},{5,4},{6,5},{7,6},{8,7},{9,8},{10,9... | collective-permute-start | bytes 1769480 | tf_op jit(solution)/shard_map/ppermute | solution.py:16
  129.4 11.2 %collective-permute-start.11 = (bf16[18,128,128]{2,1,0:T(8,128)(2,1)S(1)}, bf16[18,128,128]{2,1,0:T(8,128)(2,1)S(1)}, u32[]{:S(2)}, u32[]{:S(2)}) collective-permute-start(bf16[18,128,128]{2,1,0:T(8,128)(2,1)S(1)} %collective-permute-done.7), channel_id=1, source_target_pairs={{0,992},{32,0},{64,32},{96,64},{128,96},{160,128},{192,160},{224,1... | collective-permute-start | bytes 1769480 | tf_op jit(solution)/shard_map/ppermute | solution.py:16
where the time goes:
time: 265 us
  blocking collectives  115 us (43%)
  starting transfers between devices  68.1 us (26%)
  waiting for transfers between devices  49.4 us (19%)
  matrix products  15.7 us (6%)
  local copies, waits for them, and re-layouts  11 us (4%)
  between operations  5.2 us (2%)
    psum x1, blocking collectives, body(): totals = lax.psum((diagonal_sum, square_sum), ('row', 'col'))  115 us
    ppermute x12, starting transfers between devices, shifted(): return lax.ppermute(value, axis, pairs)  68.1 us
    ppermute x12, waiting for transfers between devices, shifted(): return lax.ppermute(value, axis, pairs)  49.4 us
    transpose x8, local copies, waits for them, and re-layouts, densify(): placed.reshape(TB, TB, BLK, BLK).transpose(0, 2, 1, 3)  8.86 us
    dot_general x4, matrix products, multiply(): jnp.dot(left_matrix, right_matrix, preferred_element_type=jnp.float32)  7.97 us
    dot_general x8, matrix products, densify(): jnp.einsum('ps,sab->pab', onehot, blocks, preferred_element_type=jnp.floa...  7.7 us
  transfers between devices with their start and end apart: 12, of which 4 were waited for; matrix products, arithmetic and copies ran while one was open for 8% of the time, Pallas kernels for 0%

commit v1 on v0

v1 whole, which is shorter than its diff:
```python
import functools
import math

import jax
import jax.numpy as jnp
from jax import lax
from jax.experimental import pallas as pl
from jax.experimental.pallas import tpu as pltpu
from jax.sharding import PartitionSpec as P

BLK = 128
TB = 6
STEPS = 4
TILE = TB * BLK
TAIL = 16
LANES = 128
BOTH = ("row", "col")


def pack_kernel(left_slots, right_slots, left, right, left_out, right_out, rows, sems):
    depth = left.shape[0]
    copies = [
        pltpu.make_async_copy(left, left_out.at[pl.ds(0, depth)], sems.at[0]),
        pltpu.make_async_copy(right, right_out.at[pl.ds(0, depth)], sems.at[1]),
    ]
    for copy in copies:
        copy.start()
    lane = lax.broadcasted_iota(jnp.int32, (TAIL, LANES), 1)
    for side, slots in enumerate((left_slots, right_slots)):
        cells = jnp.zeros((TAIL, LANES), jnp.int32)
        for slot in range(slots.shape[1]):
            cells = jnp.where(lane == slot, slots[0, slot], cells)
        rows[side] = cells.astype(jnp.float32).astype(jnp.bfloat16)
    tails = [
        pltpu.make_async_copy(rows.at[0], left_out.at[pl.ds(depth, TAIL)], sems.at[2]),
        pltpu.make_async_copy(rows.at[1], right_out.at[pl.ds(depth, TAIL)], sems.at[3]),
    ]
    for copy in tails:
        copy.start()
    for copy in copies + tails:
        copy.wait()


def pack(left_slots, right_slots, left, right):
    depth = left.shape[0]
    packed = jax.ShapeDtypeStruct((depth + TAIL, LANES), left.dtype)
    return pl.pallas_call(
        pack_kernel,
        out_shape=(packed, packed),
        in_specs=[pl.BlockSpec(memory_space=pltpu.SMEM)] * 2 + [pl.BlockSpec(memory_space=pl.ANY)] * 2,
        out_specs=(pl.BlockSpec(memory_space=pl.ANY),) * 2,
        scratch_shapes=[pltpu.VMEM((2, TAIL, LANES), left.dtype), pltpu.SemaphoreType.DMA((4,))],
        name="pack_tiles",
    )(left_slots, right_slots, left, right)


def multiply_kernel(on_diagonal, *refs):
    tiles, (out, sums, left_dense, right_dense, cells, table, sem) = refs[: 2 * STEPS], refs[2 * STEPS :]
    depth = tiles[0].shape[0] - TAIL
    slots = depth // BLK
    level = lax.broadcasted_iota(jnp.int32, (8, LANES), 0)
    gathered = jnp.zeros((8, LANES), jnp.int32)
    for index, tile in enumerate(tiles):
        tail = tile[depth : depth + TAIL, :].astype(jnp.float32).astype(jnp.int32)
        gathered = jnp.where(level == index, tail[0:8], gathered)
    cells[...] = gathered
    copy = pltpu.make_async_copy(cells, table, sem)
    copy.start()
    left_dense[...] = jnp.zeros_like(left_dense)
    right_dense[...] = jnp.zeros_like(right_dense)
    copy.wait()
    for step in range(STEPS):
        left, right = tiles[2 * step], tiles[2 * step + 1]
        for slot in range(slots):
            cell = table[2 * step, slot]
            row = pl.multiple_of(cell // TB * BLK, BLK)
            col = pl.multiple_of(step * TILE + cell % TB * BLK, BLK)
            left_dense[pl.ds(row, BLK), pl.ds(col, BLK)] = left[slot * BLK : (slot + 1) * BLK, :]
            cell = table[2 * step + 1, slot]
            row = jnp.where(cell < TB * TB, step * TILE + cell // TB * BLK, STEPS * TILE)
            row = pl.multiple_of(row, BLK)
            col = pl.multiple_of(cell % TB * BLK, BLK)
            right_dense[pl.ds(row, BLK), pl.ds(col, BLK)] = right[slot * BLK : (slot + 1) * BLK, :]
    width = 2 * BLK
    square_sum = jnp.float32(0)
    diagonal_sum = jnp.float32(0)
    inside = lax.broadcasted_iota(jnp.int32, (width, width), 0) == lax.broadcasted_iota(
        jnp.int32, (width, width), 1
    )
    for part in range(TILE // width):
        low, high = part * width, (part + 1) * width
        accum = jnp.dot(
            left_dense[0:TILE, :],
            right_dense[0 : STEPS * TILE, low:high],
            preferred_element_type=jnp.float32,
        )
        out[:, low:high] = accum.astype(out.dtype)
        square_sum += jnp.sum(accum * accum)
        diagonal_sum += jnp.sum(jnp.where(inside, accum[low:high, :], 0.0))
    diagonal_sum = jnp.where(on_diagonal[0] > 0, diagonal_sum, 0.0)
    lane = lax.broadcasted_iota(jnp.int32, sums.shape, 1)
    sums[...] = jnp.where(lane == 0, diagonal_sum, jnp.where(lane == 1, square_sum, 0.0))


def multiply(on_diagonal, tiles, fan):
    whole = pl.BlockSpec(memory_space=pltpu.VMEM)
    return pl.pallas_call(
        multiply_kernel,
        out_shape=(
            jax.ShapeDtypeStruct((TILE, TILE), jnp.bfloat16),
            jax.ShapeDtypeStruct((fan, LANES), jnp.float32),
        ),
        in_specs=[pl.BlockSpec(memory_space=pltpu.SMEM)] + [whole] * len(tiles),
        out_specs=(whole, whole),
        scratch_shapes=[
            pltpu.VMEM((TILE + BLK, STEPS * TILE), jnp.bfloat16),
            pltpu.VMEM((STEPS * TILE + BLK, TILE), jnp.bfloat16),
            pltpu.VMEM((8, LANES), jnp.int32),
            pltpu.SMEM((8, LANES), jnp.int32),
            pltpu.SemaphoreType.DMA,
        ],
        compiler_params=pltpu.CompilerParams(vmem_limit_bytes=40 * 2**20),
        cost_estimate=pl.CostEstimate(
            flops=2 * STEPS * TILE**3, bytes_accessed=8 * 600_000 + 2 * TILE * TILE, transcendentals=0
        ),
        name="place_and_multiply",
    )(on_diagonal, *tiles)


def exchange(value, target, rows, cols):
    pairs = []
    for i in range(rows):
        for j in range(cols):
            to_row, to_col = target(i, j)
            pairs.append((i * cols + j, to_row % rows * cols + to_col % cols))
    return lax.ppermute(value, BOTH, pairs)


def spread_sum(values, axis):
    return lax.all_to_all(values, axis, 0, 0, tiled=True)


def body(left_blocks, left_slots, right_blocks, right_slots):
    rows, cols = lax.axis_size("row"), lax.axis_size("col")
    on_diagonal = (lax.axis_index("row") == lax.axis_index("col")).astype(jnp.int32).reshape(1)
    left, right = pack(
        left_slots, right_slots, left_blocks.reshape(-1, LANES), right_blocks.reshape(-1, LANES)
    )
    move = functools.partial(exchange, rows=rows, cols=cols)
    left_first = move(left, lambda i, j: (i, j - 1 if i % 2 == 0 else j - 3))
    left_second = move(left, lambda i, j: (i, j - 3 if i % 2 == 0 else j - 1))
    left_middle = move(left_first, lambda i, j: (i, j - 1 if i % 2 == 0 else j + 1))
    right_middle = move(right, lambda i, j: (i - 2, j))
    right_first = move(right, lambda i, j: (i - 1 if i % 2 else i - 3, j))
    right_second = move(right_middle, lambda i, j: (i ^ 1, j))
    tiles = (left, right, left_first, right_first, left_second, right_second, left_middle, right_middle)
    product, partial = multiply(on_diagonal, tiles, rows)
    row_sums = jnp.sum(spread_sum(partial, "row"), axis=0, keepdims=True)
    totals = jnp.sum(spread_sum(jnp.broadcast_to(row_sums, (cols, LANES)), "col"), axis=0)
    trace_scaled = totals[0] / math.sqrt(min(rows, cols) * TILE)
    norm_scaled = totals[1] / (rows * cols * TILE * TILE)
    return product, trace_scaled, norm_scaled


def solution(mesh):
    placed = (
        P("row", "col", None, None),
        P("row", "col"),
        P("row", "col", None, None),
        P("row", "col"),
    )
    return jax.shard_map(
        body, mesh=mesh, in_specs=placed, out_specs=(P("row", "col"), P(), P()), check_vma=False
    )
```

time: 265 us -> 161 us (0.61)
  blocking collectives: 115 us -> 40.1 us
  Pallas kernels: 0 us -> 46.1 us
  waiting for transfers between devices: 49.4 us -> 23.8 us
  starting transfers between devices: 68.1 us -> 43.1 us
  matrix products: 15.7 us -> 0 us
  local copies, waits for them, and re-layouts: 11 us -> 2.73 us
    psum x1 -> x0, blocking collectives: 115 us -> none  [body(): totals = lax.psum((diagonal_sum, square_sum), ('row', 'col'))]
    pallas_call x0 -> x2, Pallas kernels: none -> 46.1 us  [the longest x1 37.5 us: pack(): pl.pallas_call(pack_kernel, out_shape=(packed, packed), in_specs=[pl.Bloc...]
    all_to_all x0 -> x2, blocking collectives: none -> 40.1 us  [spread_sum(): return lax.all_to_all(values, axis, 0, 0, tiled=True)]
    ppermute x12 -> x6, waiting for transfers between devices: 49.4 us -> 23.8 us  [exchange(): return lax.ppermute(value, BOTH, pairs)]
    ppermute x12 -> x6, starting transfers between devices: 68.1 us -> 43.1 us  [exchange(): return lax.ppermute(value, BOTH, pairs)]
    dot_general x12 -> x0, matrix products: 15.7 us -> none  [the longest x4 7.97 us: multiply(): jnp.dot(left_matrix, right_matrix, preferred_element_type=jnp.float32)]
    transpose x8 -> x0, local copies, waits for them, and re-layouts: 8.86 us -> none  [densify(): placed.reshape(TB, TB, BLK, BLK).transpose(0, 2, 1, 3)]
  transfers between devices with their start and end apart: 12 -> 6, of which waited for: 4 -> 2; matrix products, arithmetic and copies ran while one was open for 8% -> 0% of each run, Pallas kernels for 0% -> 0%
where the time goes in v1:
time: 161 us; the launch traced here: 160 us
  Pallas kernels  46.1 us (29%)
  starting transfers between devices  43.1 us (27%)
  blocking collectives  40.1 us (25%)
  waiting for transfers between devices  23.8 us (15%)
  between operations  4.28 us (3%)
  local copies, waits for them, and re-layouts  2.73 us (2%)
    ppermute x6, starting transfers between devices, exchange(): return lax.ppermute(value, BOTH, pairs)  43.1 us
    all_to_all x2, blocking collectives, spread_sum(): return lax.all_to_all(values, axis, 0, 0, tiled=True)  40.1 us
    pallas_call x1, Pallas kernels, pack(): pl.pallas_call(pack_kernel, out_shape=(packed, packed), in_specs=[pl.Bloc...  37.5 us
    ppermute x6, waiting for transfers between devices, exchange(): return lax.ppermute(value, BOTH, pairs)  23.8 us
    pallas_call x1, Pallas kernels, multiply(): pl.pallas_call(multiply_kernel, out_shape=(jax.ShapeDtypeStruct((TILE, TI...  8.52 us
  transfers between devices with their start and end apart: 6, of which 2 were waited for; matrix products, arithmetic and copies ran while one was open for 0% of the time, Pallas kernels for 0%

profile of v1, /device:TPU:1, one launch (start us, length us, event | category | flops | bytes accessed | tf_op | source)
XLA Modules:
  0.0 160.1 jit_solution(12955261556954297825)
XLA Ops:
  0.6 37.5 %pack_tiles.1 = (bf16[2320,128]{1,0:T(8,128)(2,1)}, bf16[2320,128]{1,0:T(8,128)(2,1)}) custom-call(s32[1,18]{1,0:T(1,128)} %left_slots.1, s32[1,18]{1,0:T(1,128)} %right_slots.1, bf16[2304,128]{1,0:T(8,128)(2,1)} %bitcast.10, bf16[2304,128]{1,0:T(8,128)(2,1)} %bitcast.11), custom_call_target="tpu_custom_call" | custom-call | tf_op jit(solution)/shard_map/pack_tiles/pallas_call | solution.py:47
  38.2 7.6 %collective-permute-start = (bf16[2320,128]{1,0:T(8,128)(2,1)}, bf16[2320,128]{1,0:T(8,128)(2,1)S(1)}, u32[]{:S(2)}, u32[]{:S(2)}) collective-permute-start(bf16[2320,128]{1,0:T(8,128)(2,1)} %get-tuple-element.7.refs_0_), channel_id=1, source_target_pairs={{0,31},{1,0},{2,1},{3,2},{4,3},{5,4},{6,5},{7,6},{8,7},{9,8},{10,9... | collective-permute-start | bytes 1781768 | tf_op jit(solution)/shard_map/ppermute | solution.py:136
  45.8 18.2 %collective-permute-start.3 = (bf16[2320,128]{1,0:T(8,128)(2,1)}, bf16[2320,128]{1,0:T(8,128)(2,1)S(1)}, u32[]{:S(2)}, u32[]{:S(2)}) collective-permute-start(bf16[2320,128]{1,0:T(8,128)(2,1)} %get-tuple-element.8.refs_1_), channel_id=1, source_target_pairs={{0,960},{1,961},{2,962},{3,963},{4,964},{5,965},{6,966},{7,967},{8... | collective-permute-start | bytes 1781768 | tf_op jit(solution)/shard_map/ppermute | solution.py:136
  63.9 3.1 %collective-permute-start.2 = (bf16[2320,128]{1,0:T(8,128)(2,1)}, bf16[2320,128]{1,0:T(8,128)(2,1)S(1)}, u32[]{:S(2)}, u32[]{:S(2)}) collective-permute-start(bf16[2320,128]{1,0:T(8,128)(2,1)} %get-tuple-element.7.refs_0_), channel_id=1, source_target_pairs={{0,29},{1,30},{2,31},{3,0},{4,1},{5,2},{6,3},{7,4},{8,5},{9,6},{10... | collective-permute-start | bytes 1781768 | tf_op jit(solution)/shard_map/ppermute | solution.py:136
  67.1 1.2 collective-permute-start.1
  68.3 0.0 collective-permute-done.refs_2_
  68.3 4.5 %collective-permute-start.5 = (bf16[2320,128]{1,0:T(8,128)(2,1)S(1)}, bf16[2320,128]{1,0:T(8,128)(2,1)S(1)}, u32[]{:S(2)}, u32[]{:S(2)}) collective-permute-start(bf16[2320,128]{1,0:T(8,128)(2,1)S(1)} %collective-permute-done.refs_2_), channel_id=1, source_target_pairs={{0,31},{1,0},{2,1},{3,2},{4,3},{5,4},{6,5},{7,6},{8,7},{9,8},{10,9... | collective-permute-start | bytes 1781768 | tf_op jit(solution)/shard_map/ppermute | solution.py:136
  72.9 22.1 %collective-permute-done.3.refs_7_ = bf16[2320,128]{1,0:T(8,128)(2,1)S(1)} collective-permute-done((bf16[2320,128]{1,0:T(8,128)(2,1)}, bf16[2320,128]{1,0:T(8,128)(2,1)S(1)}, u32[]{:S(2)}, u32[]{:S(2)}) %collective-permute-start.3) | collective-permute-done | bytes 593952 | tf_op jit(solution)/shard_map/ppermute | solution.py:136
  94.9 8.4 %collective-permute-start.4 = (bf16[2320,128]{1,0:T(8,128)(2,1)S(1)}, bf16[2320,128]{1,0:T(8,128)(2,1)}, u32[]{:S(2)}, u32[]{:S(2)}) collective-permute-start(bf16[2320,128]{1,0:T(8,128)(2,1)S(1)} %collective-permute-done.3.refs_7_), channel_id=1, source_target_pairs={{0,32},{1,33},{2,34},{3,35},{4,36},{5,37},{6,38},{7,39},{8,40},{9,... | collective-permute-start | bytes 1781768 | tf_op jit(solution)/shard_map/ppermute | solution.py:136
  103.4 0.0 collective-permute-done.2.refs_4_
  103.4 0.0 collective-permute-done.1.refs_3_
  103.4 0.0 collective-permute-done.5.refs_6_
  103.4 1.7 %collective-permute-done.4.refs_5_ = bf16[2320,128]{1,0:T(8,128)(2,1)} collective-permute-done((bf16[2320,128]{1,0:T(8,128)(2,1)S(1)}, bf16[2320,128]{1,0:T(8,128)(2,1)}, u32[]{:S(2)}, u32[]{:S(2)}) %collective-permute-start.4) | collective-permute-done | bytes 593952 | tf_op jit(solution)/shard_map/ppermute | solution.py:136
  105.1 0.0 copy-start
  105.1 1.1 copy-done
  106.2 0.0 copy-start.1
  106.2 1.1 copy-done.1
  107.3 8.5 %place_and_multiply.1 = (bf16[768,768]{1,0:T(8,128)(2,1)}, f32[32,128]{1,0:T(8,128)S(1)}) custom-call(s32[1]{0:T(128)} %bitcast.on_diagonal, bf16[2320,128]{1,0:T(8,128)(2,1)S(1)} %copy-done, bf16[2320,128]{1,0:T(8,128)(2,1)S(1)} %copy-done.1, bf16[2320,128]{1,0:T(8,128)(2,1)S(1)} %collective-permute-done.refs_2_, ...), custom_call_target="tpu_custom_call" | custom-call | flops 3623878656 | bytes 5979648 | tf_op jit(solution)/shard_map/place_and_multiply/pallas_call | solution.py:107
  115.8 22.9 %all_to_all.15 = f32[32,1,128]{2,1,0:T(1,128)S(1)} all-to-all(f32[32,1,128]{2,1,0:T(1,128)S(1)} %bitcast.9), channel_id=1, replica_groups=mesh['row'=32,'col'=32] {'row'}, dimensions={0} | all-to-all | bytes 32768 | tf_op jit(solution)/shard_map/all_to_all | solution.py:140
  138.7 0.1 reduce_sum.18
  138.8 17.2 %all_to_all.16 = f32[32,1,128]{2,1,0:T(1,128)S(1)} all-to-all(f32[32,1,128]{2,1,0:T(1,128)S(1)} %broadcast_in_dim.2), channel_id=1, replica_groups=mesh['row'=32,'col'=32] {'col'}, dimensions={0} | all-to-all | bytes 32768 | tf_op jit(solution)/shard_map/all_to_all | solution.py:140
  156.0 0.6 fusion
  (2 shorter events, 0.0 us)
Async XLA Ops:
  38.2 30.2 %collective-permute-start = (bf16[2320,128]{1,0:T(8,128)(2,1)}, bf16[2320,128]{1,0:T(8,128)(2,1)S(1)}, u32[]{:S(2)}, u32[]{:S(2)}) collective-permute-start(bf16[2320,128]{1,0:T(8,128)(2,1)} %get-tuple-element.7.refs_0_), channel_id=1, source_target_pairs={{0,31},{1,0},{2,1},{3,2},{4,3},{5,4},{6,5},{7,6},{8,7},{9,8},{10,9... | collective-permute-start | bytes 1781768 | tf_op jit(solution)/shard_map/ppermute | solution.py:136
  45.8 49.2 %collective-permute-start.3 = (bf16[2320,128]{1,0:T(8,128)(2,1)}, bf16[2320,128]{1,0:T(8,128)(2,1)S(1)}, u32[]{:S(2)}, u32[]{:S(2)}) collective-permute-start(bf16[2320,128]{1,0:T(8,128)(2,1)} %get-tuple-element.8.refs_1_), channel_id=1, source_target_pairs={{0,960},{1,961},{2,962},{3,963},{4,964},{5,965},{6,966},{7,967},{8... | collective-permute-start | bytes 1781768 | tf_op jit(solution)/shard_map/ppermute | solution.py:136
  63.9 39.4 %collective-permute-start.2 = (bf16[2320,128]{1,0:T(8,128)(2,1)}, bf16[2320,128]{1,0:T(8,128)(2,1)S(1)}, u32[]{:S(2)}, u32[]{:S(2)}) collective-permute-start(bf16[2320,128]{1,0:T(8,128)(2,1)} %get-tuple-element.7.refs_0_), channel_id=1, source_target_pairs={{0,29},{1,30},{2,31},{3,0},{4,1},{5,2},{6,3},{7,4},{8,5},{9,6},{10... | collective-permute-start | bytes 1781768 | tf_op jit(solution)/shard_map/ppermute | solution.py:136
  67.1 36.3 %collective-permute-start.1 = (bf16[2320,128]{1,0:T(8,128)(2,1)}, bf16[2320,128]{1,0:T(8,128)(2,1)S(1)}, u32[]{:S(2)}, u32[]{:S(2)}) collective-permute-start(bf16[2320,128]{1,0:T(8,128)(2,1)} %get-tuple-element.8.refs_1_), channel_id=1, source_target_pairs={{0,928},{1,929},{2,930},{3,931},{4,932},{5,933},{6,934},{7,935},{8... | collective-permute-start | bytes 1781768 | tf_op jit(solution)/shard_map/ppermute | solution.py:136
  68.3 35.1 %collective-permute-start.5 = (bf16[2320,128]{1,0:T(8,128)(2,1)S(1)}, bf16[2320,128]{1,0:T(8,128)(2,1)S(1)}, u32[]{:S(2)}, u32[]{:S(2)}) collective-permute-start(bf16[2320,128]{1,0:T(8,128)(2,1)S(1)} %collective-permute-done.refs_2_), channel_id=1, source_target_pairs={{0,31},{1,0},{2,1},{3,2},{4,3},{5,4},{6,5},{7,6},{8,7},{9,8},{10,9... | collective-permute-start | bytes 1781768 | tf_op jit(solution)/shard_map/ppermute | solution.py:136
  94.9 10.2 %collective-permute-start.4 = (bf16[2320,128]{1,0:T(8,128)(2,1)S(1)}, bf16[2320,128]{1,0:T(8,128)(2,1)}, u32[]{:S(2)}, u32[]{:S(2)}) collective-permute-start(bf16[2320,128]{1,0:T(8,128)(2,1)S(1)} %collective-permute-done.3.refs_7_), channel_id=1, source_target_pairs={{0,32},{1,33},{2,34},{3,35},{4,36},{5,37},{6,38},{7,39},{8,40},{9,... | collective-permute-start | bytes 1781768 | tf_op jit(solution)/shard_map/ppermute | solution.py:136
  105.1 1.1 copy-start
  106.2 1.1 copy-start.1

commit v2 on v1

v2 whole, which is shorter than its diff:
```python
import functools
import math

import jax
import jax.numpy as jnp
from jax import lax
from jax.experimental import pallas as pl
from jax.experimental.pallas import tpu as pltpu
from jax.sharding import PartitionSpec as P

BLK = 128
TB = 6
STEPS = 4
TILE = TB * BLK
TAIL = 16
LANES = 128
BOTH = ("row", "col")


def pack_kernel(left_slots, right_slots, left, right, left_out, right_out, sems):
    depth = left.shape[0]
    sides = ((left_slots, left, left_out), (right_slots, right, right_out))
    copies = []
    for side, (_, source, out) in enumerate(sides):
        copies.append(pltpu.make_async_copy(source, out.at[pl.ds(0, depth)], sems.at[side]))
        copies[-1].start()
    lane = lax.broadcasted_iota(jnp.int32, (TAIL, LANES), 1)
    for slots, _, out in sides:
        cells = jnp.zeros((TAIL, LANES), jnp.int32)
        for slot in range(slots.shape[1]):
            cells = jnp.where(lane == slot, slots[0, slot], cells)
        out[depth : depth + TAIL, :] = cells.astype(jnp.float32).astype(out.dtype)
    for copy in copies:
        copy.wait()


def pack(left_slots, right_slots, left, right):
    depth = left.shape[0]
    packed = jax.ShapeDtypeStruct((depth + TAIL, LANES), left.dtype)
    return pl.pallas_call(
        pack_kernel,
        out_shape=(packed, packed),
        in_specs=[pl.BlockSpec(memory_space=pltpu.SMEM)] * 2 + [pl.BlockSpec(memory_space=pl.ANY)] * 2,
        out_specs=(pl.BlockSpec(memory_space=pltpu.VMEM),) * 2,
        scratch_shapes=[pltpu.SemaphoreType.DMA((2,))],
        name="pack_tiles",
    )(left_slots, right_slots, left, right)


def gather_cells(tiles, cells, table, sem):
    depth = tiles[0].shape[0] - TAIL
    level = lax.broadcasted_iota(jnp.int32, cells.shape, 0)
    gathered = jnp.zeros(cells.shape, jnp.int32)
    for index, tile in enumerate(tiles):
        tail = tile[depth : depth + TAIL, :].astype(jnp.float32).astype(jnp.int32)
        gathered = jnp.where(level == index, tail[0 : cells.shape[0]], gathered)
    cells[...] = gathered
    copy = pltpu.make_async_copy(cells, table, sem)
    copy.start()
    return copy


def place(tile, table, index, dense, base, side):
    for slot in range((tile.shape[0] - TAIL) // BLK):
        cell = table[index, slot]
        row, col = cell // TB * BLK, cell % TB * BLK
        if side == "left":
            col = base + col
        else:
            row = jnp.where(cell < TB * TB, base + row, dense.shape[0] - BLK)
        row, col = pl.multiple_of(row, BLK), pl.multiple_of(col, BLK)
        dense[pl.ds(row, BLK), pl.ds(col, BLK)] = tile[slot * BLK : (slot + 1) * BLK, :]


def early_kernel(left_0, right_0, left_1, right_1, right_2, right_3, accum, later, left_dense, right_dense, cells, table, sem):
    tiles = (left_0, right_0, left_1, right_1, right_2, right_3)
    copy = gather_cells(tiles, cells, table, sem)
    for dense in (left_dense, right_dense, later):
        dense[...] = jnp.zeros_like(dense)
    copy.wait()
    place(left_0, table, 0, left_dense, 0, "left")
    place(right_0, table, 1, right_dense, 0, "right")
    place(left_1, table, 2, left_dense, TILE, "left")
    place(right_1, table, 3, right_dense, TILE, "right")
    place(right_2, table, 4, later, 0, "right")
    place(right_3, table, 5, later, TILE, "right")
    for low in range(0, TILE, 2 * BLK):
        accum[:, low : low + 2 * BLK] = jnp.dot(
            left_dense[0:TILE, :],
            right_dense[0 : 2 * TILE, low : low + 2 * BLK],
            preferred_element_type=jnp.float32,
        )


def late_kernel(on_diagonal, accum, right_dense, left_2, left_3, out, sums, left_dense, cells, table, sem):
    copy = gather_cells((left_2, left_3), cells, table, sem)
    left_dense[...] = jnp.zeros_like(left_dense)
    copy.wait()
    place(left_2, table, 0, left_dense, 0, "left")
    place(left_3, table, 1, left_dense, TILE, "left")
    width = 2 * BLK
    square_sum = jnp.float32(0)
    diagonal_sum = jnp.float32(0)
    inside = lax.broadcasted_iota(jnp.int32, (width, width), 0) == lax.broadcasted_iota(
        jnp.int32, (width, width), 1
    )
    for low in range(0, TILE, width):
        total = accum[:, low : low + width] + jnp.dot(
            left_dense[0:TILE, :],
            right_dense[0 : 2 * TILE, low : low + width],
            preferred_element_type=jnp.float32,
        )
        out[:, low : low + width] = total.astype(out.dtype)
        square_sum += jnp.sum(total * total)
        diagonal_sum += jnp.sum(jnp.where(inside, total[low : low + width, :], 0.0))
    diagonal_sum = jnp.where(on_diagonal[0] > 0, diagonal_sum, 0.0)
    lane = lax.broadcasted_iota(jnp.int32, sums.shape, 1)
    sums[...] = jnp.where(lane == 0, diagonal_sum, jnp.where(lane == 1, square_sum, 0.0))


WHOLE = pl.BlockSpec(memory_space=pltpu.VMEM)
LEFT_PAIR = pltpu.VMEM((TILE + BLK, 2 * TILE), jnp.bfloat16)
RIGHT_PAIR = (2 * TILE + BLK, TILE)
CELLS = [pltpu.VMEM((8, LANES), jnp.int32), pltpu.SMEM((8, LANES), jnp.int32), pltpu.SemaphoreType.DMA]


def multiply_early(tiles):
    return pl.pallas_call(
        early_kernel,
        out_shape=(
            jax.ShapeDtypeStruct((TILE, TILE), jnp.float32),
            jax.ShapeDtypeStruct(RIGHT_PAIR, jnp.bfloat16),
        ),
        in_specs=[WHOLE] * len(tiles),
        out_specs=(WHOLE, WHOLE),
        scratch_shapes=[LEFT_PAIR, pltpu.VMEM(RIGHT_PAIR, jnp.bfloat16)] + CELLS,
        compiler_params=pltpu.CompilerParams(vmem_limit_bytes=24 * 2**20),
        cost_estimate=pl.CostEstimate(flops=4 * TILE**3, bytes_accessed=10_000_000, transcendentals=0),
        name="first_two_products",
    )(*tiles)


def multiply_late(on_diagonal, accum, right_dense, tiles, fan):
    return pl.pallas_call(
        late_kernel,
        out_shape=(
            jax.ShapeDtypeStruct((TILE, TILE), jnp.bfloat16),
            jax.ShapeDtypeStruct((fan, LANES), jnp.float32),
        ),
        in_specs=[pl.BlockSpec(memory_space=pltpu.SMEM)] + [WHOLE] * 4,
        out_specs=(WHOLE, WHOLE),
        scratch_shapes=[LEFT_PAIR] + CELLS,
        compiler_params=pltpu.CompilerParams(vmem_limit_bytes=24 * 2**20),
        cost_estimate=pl.CostEstimate(flops=4 * TILE**3, bytes_accessed=8_000_000, transcendentals=0),
        name="last_two_products",
    )(on_diagonal, accum, right_dense, *tiles)


def exchange(value, target, rows, cols):
    pairs = []
    for i in range(rows):
        for j in range(cols):
            to_row, to_col = target(i, j)
            pairs.append((i * cols + j, to_row % rows * cols + to_col % cols))
    return lax.ppermute(value, BOTH, pairs)


def spread_sum(values, axis):
    return lax.all_to_all(values, axis, 0, 0, tiled=True)


def body(left_blocks, left_slots, right_blocks, right_slots):
    rows, cols = lax.axis_size("row"), lax.axis_size("col")
    on_diagonal = (lax.axis_index("row") == lax.axis_index("col")).astype(jnp.int32).reshape(1)
    left, right = pack(
        left_slots, right_slots, left_blocks.reshape(-1, LANES), right_blocks.reshape(-1, LANES)
    )
    move = functools.partial(exchange, rows=rows, cols=cols)
    right_middle = move(right, lambda i, j: (i - 2, j))
    left_first = move(left, lambda i, j: (i, j - 1 if i % 2 == 0 else j - 3))
    left_second = move(left, lambda i, j: (i, j - 3 if i % 2 == 0 else j - 1))
    left_middle = move(left_first, lambda i, j: (i, j - 1 if i % 2 == 0 else j + 1))
    right_first = move(right, lambda i, j: (i - 1 if i % 2 else i - 3, j))
    right_second = move(right_middle, lambda i, j: (i ^ 1, j))
    accum, later = multiply_early((left, right, left_first, right_first, right_second, right_middle))
    product, partial = multiply_late(on_diagonal, accum, later, (left_second, left_middle), rows)
    row_sums = jnp.sum(spread_sum(partial, "row"), axis=0, keepdims=True)
    totals = jnp.sum(spread_sum(jnp.broadcast_to(row_sums, (cols, LANES)), "col"), axis=0)
    trace_scaled = totals[0] / math.sqrt(min(rows, cols) * TILE)
    norm_scaled = totals[1] / (rows * cols * TILE * TILE)
    return product, trace_scaled, norm_scaled


def solution(mesh):
    placed = (
        P("row", "col", None, None),
        P("row", "col"),
        P("row", "col", None, None),
        P("row", "col"),
    )
    return jax.shard_map(
        body, mesh=mesh, in_specs=placed, out_specs=(P("row", "col"), P(), P()), check_vma=False
    )
```

time: 161 us -> 125 us (0.78)
  Pallas kernels: 46.1 us -> 12.1 us
  starting transfers between devices: 43.1 us -> 38 us
  blocking collectives: 40.1 us -> 44.8 us
    pallas_call x1, Pallas kernels: 37.5 us -> 2.95 us  [pack(): pl.pallas_call(pack_kernel, out_shape=(packed, packed), in_specs=[pl.Bloc...]
    ppermute x6, starting transfers between devices: 43.1 us -> 38 us  [exchange(): return lax.ppermute(value, BOTH, pairs)]
    all_to_all x2, blocking collectives: 40.1 us -> 44.8 us  [spread_sum(): return lax.all_to_all(values, axis, 0, 0, tiled=True)]
    pallas_call x1 -> x2, Pallas kernels: 8.52 us -> 9.13 us  [the longest x1 5.05 us: multiply_early(): pl.pallas_call(early_kernel, out_shape=(jax.ShapeDtypeStruct((TILE, TILE)...]
  transfers between devices with their start and end apart: 6 -> 6, of which waited for: 2 -> 3; matrix products, arithmetic and copies ran while one was open for 0% -> 0% of each run, Pallas kernels for 0% -> 4%
where the time goes in v2:
time: 125 us; the launch traced here: 124 us
  blocking collectives  44.8 us (36%)
  starting transfers between devices  38 us (30%)
  waiting for transfers between devices  22.5 us (18%)
  Pallas kernels  12.1 us (10%)
  between operations  4.29 us (3%)
  local copies, waits for them, and re-layouts  2.73 us (2%)
    all_to_all x2, blocking collectives, spread_sum(): return lax.all_to_all(values, axis, 0, 0, tiled=True)  44.8 us
    ppermute x6, starting transfers between devices, exchange(): return lax.ppermute(value, BOTH, pairs)  38 us
    ppermute x6, waiting for transfers between devices, exchange(): return lax.ppermute(value, BOTH, pairs)  22.5 us
    pallas_call x1, Pallas kernels, multiply_early(): pl.pallas_call(early_kernel, out_shape=(jax.ShapeDtypeStruct((TILE, TILE)...  5.05 us
    pallas_call x1, Pallas kernels, multiply_late(): pl.pallas_call(late_kernel, out_shape=(jax.ShapeDtypeStruct((TILE, TILE),...  4.08 us
    pallas_call x1, Pallas kernels, pack(): pl.pallas_call(pack_kernel, out_shape=(packed, packed), in_specs=[pl.Bloc...  2.95 us
  transfers between devices with their start and end apart: 6, of which 3 were waited for; matrix products, arithmetic and copies ran while one was open for 0% of the time, Pallas kernels for 4%

profile of v2, /device:TPU:1, one launch (start us, length us, event | category | flops | bytes accessed | tf_op | source)
XLA Modules:
  0.0 124.4 jit_solution(138530154619452477)
XLA Ops:
  0.6 2.9 %pack_tiles.1 = (bf16[2320,128]{1,0:T(8,128)(2,1)}, bf16[2320,128]{1,0:T(8,128)(2,1)}) custom-call(s32[1,18]{1,0:T(1,128)} %left_slots.1, s32[1,18]{1,0:T(1,128)} %right_slots.1, bf16[2304,128]{1,0:T(8,128)(2,1)} %bitcast.10, bf16[2304,128]{1,0:T(8,128)(2,1)} %bitcast.11), custom_call_target="tpu_custom_call" | custom-call | tf_op jit(solution)/shard_map/pack_tiles/pallas_call | solution.py:40
  3.6 19.0 %collective-permute-start.2 = (bf16[2320,128]{1,0:T(8,128)(2,1)}, bf16[2320,128]{1,0:T(8,128)(2,1)S(1)}, u32[]{:S(2)}, u32[]{:S(2)}) collective-permute-start(bf16[2320,128]{1,0:T(8,128)(2,1)} %get-tuple-element.10.right_0), channel_id=1, source_target_pairs={{0,960},{1,961},{2,962},{3,963},{4,964},{5,965},{6,966},{7,967},{8... | collective-permute-start | bytes 1781768 | tf_op jit(solution)/shard_map/ppermute | solution.py:165
  22.6 6.8 %collective-permute-start = (bf16[2320,128]{1,0:T(8,128)(2,1)}, bf16[2320,128]{1,0:T(8,128)(2,1)S(1)}, u32[]{:S(2)}, u32[]{:S(2)}) collective-permute-start(bf16[2320,128]{1,0:T(8,128)(2,1)} %get-tuple-element.9.left_0), channel_id=1, source_target_pairs={{0,31},{1,0},{2,1},{3,2},{4,3},{5,4},{6,5},{7,6},{8,7},{9,8},{10,9... | collective-permute-start | bytes 1781768 | tf_op jit(solution)/shard_map/ppermute | solution.py:165
  29.3 2.5 %collective-permute-start.1 = (bf16[2320,128]{1,0:T(8,128)(2,1)}, bf16[2320,128]{1,0:T(8,128)(2,1)S(1)}, u32[]{:S(2)}, u32[]{:S(2)}) collective-permute-start(bf16[2320,128]{1,0:T(8,128)(2,1)} %get-tuple-element.10.right_0), channel_id=1, source_target_pairs={{0,928},{1,929},{2,930},{3,931},{4,932},{5,933},{6,934},{7,935},{8... | collective-permute-start | bytes 1781768 | tf_op jit(solution)/shard_map/ppermute | solution.py:165
  31.8 9.6 %collective-permute-done.2.right_3 = bf16[2320,128]{1,0:T(8,128)(2,1)S(1)} collective-permute-done((bf16[2320,128]{1,0:T(8,128)(2,1)}, bf16[2320,128]{1,0:T(8,128)(2,1)S(1)}, u32[]{:S(2)}, u32[]{:S(2)}) %collective-permute-start.2) | collective-permute-done | bytes 593952 | tf_op jit(solution)/shard_map/ppermute | solution.py:165
  41.4 3.4 %collective-permute-start.3 = (bf16[2320,128]{1,0:T(8,128)(2,1)S(1)}, bf16[2320,128]{1,0:T(8,128)(2,1)}, u32[]{:S(2)}, u32[]{:S(2)}) collective-permute-start(bf16[2320,128]{1,0:T(8,128)(2,1)S(1)} %collective-permute-done.2.right_3), channel_id=1, source_target_pairs={{0,32},{1,33},{2,34},{3,35},{4,36},{5,37},{6,38},{7,39},{8,40},{9,... | collective-permute-start | bytes 1781768 | tf_op jit(solution)/shard_map/ppermute | solution.py:165
  44.8 2.8 %collective-permute-start.4 = (bf16[2320,128]{1,0:T(8,128)(2,1)}, bf16[2320,128]{1,0:T(8,128)(2,1)S(1)}, u32[]{:S(2)}, u32[]{:S(2)}) collective-permute-start(bf16[2320,128]{1,0:T(8,128)(2,1)} %get-tuple-element.9.left_0), channel_id=1, source_target_pairs={{0,29},{1,30},{2,31},{3,0},{4,1},{5,2},{6,3},{7,4},{8,5},{9,6},{10... | collective-permute-start | bytes 1781768 | tf_op jit(solution)/shard_map/ppermute | solution.py:165
  47.6 0.0 collective-permute-done.left_1
  47.6 3.6 %collective-permute-start.5 = (bf16[2320,128]{1,0:T(8,128)(2,1)S(1)}, bf16[2320,128]{1,0:T(8,128)(2,1)S(1)}, u32[]{:S(2)}, u32[]{:S(2)}) collective-permute-start(bf16[2320,128]{1,0:T(8,128)(2,1)S(1)} %collective-permute-done.left_1), channel_id=1, source_target_pairs={{0,31},{1,0},{2,1},{3,2},{4,3},{5,4},{6,5},{7,6},{8,7},{9,8},{10,9... | collective-permute-start | bytes 1781768 | tf_op jit(solution)/shard_map/ppermute | solution.py:165
  51.2 0.0 collective-permute-done.1.right_1
  51.2 0.0 collective-permute-done.3.right_2
  51.2 0.0 copy-start
  51.3 1.1 copy-done
  52.3 0.0 copy-start.1
  52.3 1.1 copy-done.1
  53.4 5.1 %first_two_products.1 = (f32[768,768]{1,0:T(8,128)S(1)}, bf16[1664,768]{1,0:T(8,128)(2,1)S(1)}) custom-call(bf16[2320,128]{1,0:T(8,128)(2,1)S(1)} %copy-done, bf16[2320,128]{1,0:T(8,128)(2,1)S(1)} %copy-done.1, bf16[2320,128]{1,0:T(8,128)(2,1)S(1)} %collective-permute-done.left_1, bf16[2320,128]{1,0:T(8,128)(2,1)S(1)} %collective-permute-done.1.right_1, ...), custom_call_target="tpu_custom_call" | custom-call | flops 1811939328 | bytes 10000000 | tf_op jit(solution)/shard_map/first_two_products/pallas_call | solution.py:128
  58.4 9.6 %collective-permute-done.4.left_2 = bf16[2320,128]{1,0:T(8,128)(2,1)S(1)} collective-permute-done((bf16[2320,128]{1,0:T(8,128)(2,1)}, bf16[2320,128]{1,0:T(8,128)(2,1)S(1)}, u32[]{:S(2)}, u32[]{:S(2)}) %collective-permute-start.4) | collective-permute-done | bytes 593952 | tf_op jit(solution)/shard_map/ppermute | solution.py:165
  68.1 3.3 %collective-permute-done.5.left_3 = bf16[2320,128]{1,0:T(8,128)(2,1)S(1)} collective-permute-done((bf16[2320,128]{1,0:T(8,128)(2,1)S(1)}, bf16[2320,128]{1,0:T(8,128)(2,1)S(1)}, u32[]{:S(2)}, u32[]{:S(2)}) %collective-permute-start.5) | collective-permute-done | bytes 593952 | tf_op jit(solution)/shard_map/ppermute | solution.py:165
  71.4 4.1 %last_two_products.1 = (bf16[768,768]{1,0:T(8,128)(2,1)}, f32[32,128]{1,0:T(8,128)S(1)}) custom-call(s32[1]{0:T(128)} %bitcast.on_diagonal, f32[768,768]{1,0:T(8,128)S(1)} %get-tuple-element.11.accum, bf16[1664,768]{1,0:T(8,128)(2,1)S(1)} %get-tuple-element.12.right_dense, bf16[2320,128]{1,0:T(8,128)(2,1)S(1)} %collective-permute-done.4.left_2, ...), custom_call_target="tpu_custom_call" | custom-call | flops 1811939328 | bytes 8000000 | tf_op jit(solution)/shard_map/last_two_products/pallas_call | solution.py:144
  75.4 24.4 %all_to_all.15 = f32[32,1,128]{2,1,0:T(1,128)S(1)} all-to-all(f32[32,1,128]{2,1,0:T(1,128)S(1)} %bitcast.9), channel_id=1, replica_groups=mesh['row'=32,'col'=32] {'row'}, dimensions={0} | all-to-all | bytes 32768 | tf_op jit(solution)/shard_map/all_to_all | solution.py:169
  99.9 0.1 reduce_sum.18
  99.9 20.3 %all_to_all.16 = f32[32,1,128]{2,1,0:T(1,128)S(1)} all-to-all(f32[32,1,128]{2,1,0:T(1,128)S(1)} %broadcast_in_dim.2), channel_id=1, replica_groups=mesh['row'=32,'col'=32] {'col'}, dimensions={0} | all-to-all | bytes 32768 | tf_op jit(solution)/shard_map/all_to_all | solution.py:169
  120.3 0.6 fusion
  (2 shorter events, 0.0 us)
Async XLA Ops:
  3.6 37.8 %collective-permute-start.2 = (bf16[2320,128]{1,0:T(8,128)(2,1)}, bf16[2320,128]{1,0:T(8,128)(2,1)S(1)}, u32[]{:S(2)}, u32[]{:S(2)}) collective-permute-start(bf16[2320,128]{1,0:T(8,128)(2,1)} %get-tuple-element.10.right_0), channel_id=1, source_target_pairs={{0,960},{1,961},{2,962},{3,963},{4,964},{5,965},{6,966},{7,967},{8... | collective-permute-start | bytes 1781768 | tf_op jit(solution)/shard_map/ppermute | solution.py:165
  22.6 25.0 %collective-permute-start = (bf16[2320,128]{1,0:T(8,128)(2,1)}, bf16[2320,128]{1,0:T(8,128)(2,1)S(1)}, u32[]{:S(2)}, u32[]{:S(2)}) collective-permute-start(bf16[2320,128]{1,0:T(8,128)(2,1)} %get-tuple-element.9.left_0), channel_id=1, source_target_pairs={{0,31},{1,0},{2,1},{3,2},{4,3},{5,4},{6,5},{7,6},{8,7},{9,8},{10,9... | collective-permute-start | bytes 1781768 | tf_op jit(solution)/shard_map/ppermute | solution.py:165
  29.3 21.9 %collective-permute-start.1 = (bf16[2320,128]{1,0:T(8,128)(2,1)}, bf16[2320,128]{1,0:T(8,128)(2,1)S(1)}, u32[]{:S(2)}, u32[]{:S(2)}) collective-permute-start(bf16[2320,128]{1,0:T(8,128)(2,1)} %get-tuple-element.10.right_0), channel_id=1, source_target_pairs={{0,928},{1,929},{2,930},{3,931},{4,932},{5,933},{6,934},{7,935},{8... | collective-permute-start | bytes 1781768 | tf_op jit(solution)/shard_map/ppermute | solution.py:165
  41.4 9.9 %collective-permute-start.3 = (bf16[2320,128]{1,0:T(8,128)(2,1)S(1)}, bf16[2320,128]{1,0:T(8,128)(2,1)}, u32[]{:S(2)}, u32[]{:S(2)}) collective-permute-start(bf16[2320,128]{1,0:T(8,128)(2,1)S(1)} %collective-permute-done.2.right_3), channel_id=1, source_target_pairs={{0,32},{1,33},{2,34},{3,35},{4,36},{5,37},{6,38},{7,39},{8,40},{9,... | collective-permute-start | bytes 1781768 | tf_op jit(solution)/shard_map/ppermute | solution.py:165
  44.8 23.3 %collective-permute-start.4 = (bf16[2320,128]{1,0:T(8,128)(2,1)}, bf16[2320,128]{1,0:T(8,128)(2,1)S(1)}, u32[]{:S(2)}, u32[]{:S(2)}) collective-permute-start(bf16[2320,128]{1,0:T(8,128)(2,1)} %get-tuple-element.9.left_0), channel_id=1, source_target_pairs={{0,29},{1,30},{2,31},{3,0},{4,1},{5,2},{6,3},{7,4},{8,5},{9,6},{10... | collective-permute-start | bytes 1781768 | tf_op jit(solution)/shard_map/ppermute | solution.py:165
  47.6 23.8 %collective-permute-start.5 = (bf16[2320,128]{1,0:T(8,128)(2,1)S(1)}, bf16[2320,128]{1,0:T(8,128)(2,1)S(1)}, u32[]{:S(2)}, u32[]{:S(2)}) collective-permute-start(bf16[2320,128]{1,0:T(8,128)(2,1)S(1)} %collective-permute-done.left_1), channel_id=1, source_target_pairs={{0,31},{1,0},{2,1},{3,2},{4,3},{5,4},{6,5},{7,6},{8,7},{9,8},{10,9... | collective-permute-start | bytes 1781768 | tf_op jit(solution)/shard_map/ppermute | solution.py:165
  51.2 1.1 copy-start
  52.3 1.1 copy-start.1

commit v3 on v2

--- a/solution.py
+++ b/solution.py
@@ -43,6 +43,7 @@
         in_specs=[pl.BlockSpec(memory_space=pltpu.SMEM)] * 2 + [pl.BlockSpec(memory_space=pl.ANY)] * 2,
         out_specs=(pl.BlockSpec(memory_space=pltpu.VMEM),) * 2,
         scratch_shapes=[pltpu.SemaphoreType.DMA((2,))],
+        compiler_params=pltpu.CompilerParams(vmem_limit_bytes=4 * 2**20),
         name="pack_tiles",
     )(left_slots, right_slots, left, right)
 
@@ -72,32 +73,29 @@
         dense[pl.ds(row, BLK), pl.ds(col, BLK)] = tile[slot * BLK : (slot + 1) * BLK, :]
 
 
-def early_kernel(left_0, right_0, left_1, right_1, right_2, right_3, accum, later, left_dense, right_dense, cells, table, sem):
-    tiles = (left_0, right_0, left_1, right_1, right_2, right_3)
-    copy = gather_cells(tiles, cells, table, sem)
+def early_kernel(left_0, right_0, left_1, right_1, left_2, right_2, right_3, accum, later, left_dense, right_dense, cells, table, sem):
+    tiles = (left_0, right_0, left_1, right_1, left_2, right_2)
+    copy = gather_cells(tiles + (right_3,), cells, table, sem)
     for dense in (left_dense, right_dense, later):
         dense[...] = jnp.zeros_like(dense)
     copy.wait()
-    place(left_0, table, 0, left_dense, 0, "left")
-    place(right_0, table, 1, right_dense, 0, "right")
-    place(left_1, table, 2, left_dense, TILE, "left")
-    place(right_1, table, 3, right_dense, TILE, "right")
-    place(right_2, table, 4, later, 0, "right")
-    place(right_3, table, 5, later, TILE, "right")
+    for step in range(EARLY):
+        place(tiles[2 * step], table, 2 * step, left_dense, step * TILE, "left")
+        place(tiles[2 * step + 1], table, 2 * step + 1, right_dense, step * TILE, "right")
+    place(right_3, table, 2 * EARLY, later, 0, "right")
     for low in range(0, TILE, 2 * BLK):
         accum[:, low : low + 2 * BLK] = jnp.dot(
             left_dense[0:TILE, :],
-            right_dense[0 : 2 * TILE, low : low + 2 * BLK],
+            right_dense[0 : EARLY * TILE, low : low + 2 * BLK],
             preferred_element_type=jnp.float32,
         )
 
 
-def late_kernel(on_diagonal, accum, right_dense, left_2, left_3, out, sums, left_dense, cells, table, sem):
-    copy = gather_cells((left_2, left_3), cells, table, sem)
+def late_kernel(on_diagonal, accum, right_dense, left_3, out, sums, left_dense, cells, table, sem):
+    copy = gather_cells((left_3,), cells, table, sem)
     left_dense[...] = jnp.zeros_like(left_dense)
     copy.wait()
-    place(left_2, table, 0, left_dense, 0, "left")
-    place(left_3, table, 1, left_dense, TILE, "left")
+    place(left_3, table, 0, left_dense, 0, "left")
     width = 2 * BLK
     square_sum = jnp.float32(0)
     diagonal_sum = jnp.float32(0)
@@ -107,7 +105,7 @@
     for low in range(0, TILE, width):
         total = accum[:, low : low + width] + jnp.dot(
             left_dense[0:TILE, :],
-            right_dense[0 : 2 * TILE, low : low + width],
+            right_dense[0:TILE, low : low + width],
             preferred_element_type=jnp.float32,
         )
         out[:, low : low + width] = total.astype(out.dtype)
@@ -119,9 +117,16 @@
 
 
 WHOLE = pl.BlockSpec(memory_space=pltpu.VMEM)
-LEFT_PAIR = pltpu.VMEM((TILE + BLK, 2 * TILE), jnp.bfloat16)
-RIGHT_PAIR = (2 * TILE + BLK, TILE)
+EARLY = STEPS - 1
 CELLS = [pltpu.VMEM((8, LANES), jnp.int32), pltpu.SMEM((8, LANES), jnp.int32), pltpu.SemaphoreType.DMA]
+
+
+def left_shape(steps):
+    return (TILE + BLK, steps * TILE)
+
+
+def right_shape(steps):
+    return (steps * TILE + BLK, TILE)
 
 
 def multiply_early(tiles):
@@ -129,31 +134,31 @@
         early_kernel,
         out_shape=(
             jax.ShapeDtypeStruct((TILE, TILE), jnp.float32),
-            jax.ShapeDtypeStruct(RIGHT_PAIR, jnp.bfloat16),
+            jax.ShapeDtypeStruct(right_shape(1), jnp.bfloat16),
         ),
         in_specs=[WHOLE] * len(tiles),
         out_specs=(WHOLE, WHOLE),
-        scratch_shapes=[LEFT_PAIR, pltpu.VMEM(RIGHT_PAIR, jnp.bfloat16)] + CELLS,
+        scratch_shapes=[pltpu.VMEM(left_shape(EARLY), jnp.bfloat16), pltpu.VMEM(right_shape(EARLY), jnp.bfloat16)] + CELLS,
         compiler_params=pltpu.CompilerParams(vmem_limit_bytes=24 * 2**20),
-        cost_estimate=pl.CostEstimate(flops=4 * TILE**3, bytes_accessed=10_000_000, transcendentals=0),
-        name="first_two_products",
+        cost_estimate=pl.CostEstimate(flops=2 * EARLY * TILE**3, bytes_accessed=10_000_000, transcendentals=0),
+        name="first_three_products",
     )(*tiles)
 
 
-def multiply_late(on_diagonal, accum, right_dense, tiles, fan):
+def multiply_late(on_diagonal, accum, right_dense, left_tile, fan):
     return pl.pallas_call(
         late_kernel,
         out_shape=(
             jax.ShapeDtypeStruct((TILE, TILE), jnp.bfloat16),
             jax.ShapeDtypeStruct((fan, LANES), jnp.float32),
         ),
-        in_specs=[pl.BlockSpec(memory_space=pltpu.SMEM)] + [WHOLE] * 4,
+        in_specs=[pl.BlockSpec(memory_space=pltpu.SMEM)] + [WHOLE] * 3,
         out_specs=(WHOLE, WHOLE),
-        scratch_shapes=[LEFT_PAIR] + CELLS,
-        compiler_params=pltpu.CompilerParams(vmem_limit_bytes=24 * 2**20),
-        cost_estimate=pl.CostEstimate(flops=4 * TILE**3, bytes_accessed=8_000_000, transcendentals=0),
-        name="last_two_products",
-    )(on_diagonal, accum, right_dense, *tiles)
+        scratch_shapes=[pltpu.VMEM(left_shape(1), jnp.bfloat16)] + CELLS,
+        compiler_params=pltpu.CompilerParams(vmem_limit_bytes=16 * 2**20),
+        cost_estimate=pl.CostEstimate(flops=2 * TILE**3, bytes_accessed=6_000_000, transcendentals=0),
+        name="last_product",
+    )(on_diagonal, accum, right_dense, left_tile)
 
 
 def exchange(value, target, rows, cols):
@@ -176,14 +181,14 @@
         left_slots, right_slots, left_blocks.reshape(-1, LANES), right_blocks.reshape(-1, LANES)
     )
     move = functools.partial(exchange, rows=rows, cols=cols)
+    left_first = move(left, lambda i, j: (i, j - 1 if i % 2 == 0 else j - 3))
     right_middle = move(right, lambda i, j: (i - 2, j))
-    left_first = move(left, lambda i, j: (i, j - 1 if i % 2 == 0 else j - 3))
     left_second = move(left, lambda i, j: (i, j - 3 if i % 2 == 0 else j - 1))
+    right_first = move(right, lambda i, j: (i - 1 if i % 2 else i - 3, j))
     left_middle = move(left_first, lambda i, j: (i, j - 1 if i % 2 == 0 else j + 1))
-    right_first = move(right, lambda i, j: (i - 1 if i % 2 else i - 3, j))
     right_second = move(right_middle, lambda i, j: (i ^ 1, j))
-    accum, later = multiply_early((left, right, left_first, right_first, right_second, right_middle))
-    product, partial = multiply_late(on_diagonal, accum, later, (left_second, left_middle), rows)
+    accum, later = multiply_early((left, right, left_first, right_first, left_second, right_second, right_middle))
+    product, partial = multiply_late(on_diagonal, accum, later, left_middle, rows)
     row_sums = jnp.sum(spread_sum(partial, "row"), axis=0, keepdims=True)
     totals = jnp.sum(spread_sum(jnp.broadcast_to(row_sums, (cols, LANES)), "col"), axis=0)
     trace_scaled = totals[0] / math.sqrt(min(rows, cols) * TILE)

time: 125 us -> 124 us (level)
  starting transfers between devices: 38 us -> 46.4 us
  blocking collectives: 44.8 us -> 39.7 us
  waiting for transfers between devices: 22.5 us -> 18.3 us
  Pallas kernels: 12.1 us -> 10.3 us
  local copies, waits for them, and re-layouts: 2.73 us -> 4.03 us
    ppermute x6, starting transfers between devices: 38 us -> 46.4 us  [exchange(): return lax.ppermute(value, BOTH, pairs)]
    all_to_all x2, blocking collectives: 44.8 us -> 39.7 us  [spread_sum(): return lax.all_to_all(values, axis, 0, 0, tiled=True)]
    ppermute x6, waiting for transfers between devices: 22.5 us -> 18.3 us  [exchange(): return lax.ppermute(value, BOTH, pairs)]
    pallas_call x1, Pallas kernels: 2.95 us -> 0.82 us  [pack(): pl.pallas_call(pack_kernel, out_shape=(packed, packed), in_specs=[pl.Bloc...]
    pallas_call x1, Pallas kernels: 5.05 us -> 6.55 us  [multiply_early(): pl.pallas_call(early_kernel, out_shape=(jax.ShapeDtypeStruct((TILE, TILE)...]
    unnamed x4 -> x8, local copies, waits for them, and re-layouts: 2.13 us -> 3.43 us
  transfers between devices with their start and end apart: 6 -> 6, of which waited for: 3 -> 3; matrix products, arithmetic and copies ran while one was open for 0% -> 0% of each run, Pallas kernels for 4% -> 5%
where the time goes in v3:
time: 124 us; the launch traced here: 123 us
  starting transfers between devices  46.4 us (37%)
  blocking collectives  39.7 us (32%)
  waiting for transfers between devices  18.3 us (15%)
  Pallas kernels  10.3 us (8%)
  between operations  4.3 us (3%)
  local copies, waits for them, and re-layouts  4.03 us (3%)
    ppermute x6, starting transfers between devices, exchange(): return lax.ppermute(value, BOTH, pairs)  46.4 us
    all_to_all x2, blocking collectives, spread_sum(): return lax.all_to_all(values, axis, 0, 0, tiled=True)  39.7 us
    ppermute x6, waiting for transfers between devices, exchange(): return lax.ppermute(value, BOTH, pairs)  18.3 us
    pallas_call x1, Pallas kernels, multiply_early(): pl.pallas_call(early_kernel, out_shape=(jax.ShapeDtypeStruct((TILE, TILE)...  6.55 us
    unnamed x8, local copies, waits for them, and re-layouts  3.43 us
    pallas_call x1, Pallas kernels, multiply_late(): pl.pallas_call(late_kernel, out_shape=(jax.ShapeDtypeStruct((TILE, TILE),...  2.94 us
  transfers between devices with their start and end apart: 6, of which 3 were waited for; matrix products, arithmetic and copies ran while one was open for 0% of the time, Pallas kernels for 5%

profile of v3, /device:TPU:1, one launch (start us, length us, event | category | flops | bytes accessed | tf_op | source)
XLA Modules:
  0.0 123.1 jit_solution(13807511493405964107)
XLA Ops:
  0.6 0.0 copy-start
  0.6 1.1 copy-done
  1.7 0.0 copy-start.1
  1.7 1.1 copy-done.1
  2.8 0.0 copy-start.2
  2.8 0.7 copy-done.2
  3.4 0.0 copy-start.3
  3.4 0.7 copy-done.3
  4.1 0.8 pack_tiles.1
  4.9 19.0 %collective-permute-start.3 = (bf16[2320,128]{1,0:T(8,128)(2,1)S(1)}, bf16[2320,128]{1,0:T(8,128)(2,1)S(1)}, u32[]{:S(2)}, u32[]{:S(2)}) collective-permute-start(bf16[2320,128]{1,0:T(8,128)(2,1)S(1)} %get-tuple-element.10.right_0), channel_id=1, source_target_pairs={{0,960},{1,961},{2,962},{3,963},{4,964},{5,965},{6,966},{7,967},{8... | collective-permute-start | bytes 1781768 | tf_op jit(solution)/shard_map/ppermute | solution.py:170
  23.9 6.8 %collective-permute-start = (bf16[2320,128]{1,0:T(8,128)(2,1)S(1)}, bf16[2320,128]{1,0:T(8,128)(2,1)S(1)}, u32[]{:S(2)}, u32[]{:S(2)}) collective-permute-start(bf16[2320,128]{1,0:T(8,128)(2,1)S(1)} %get-tuple-element.9.left_0), channel_id=1, source_target_pairs={{0,31},{1,0},{2,1},{3,2},{4,3},{5,4},{6,5},{7,6},{8,7},{9,8},{10,9... | collective-permute-start | bytes 1781768 | tf_op jit(solution)/shard_map/ppermute | solution.py:170
  30.7 2.5 %collective-permute-start.1 = (bf16[2320,128]{1,0:T(8,128)(2,1)S(1)}, bf16[2320,128]{1,0:T(8,128)(2,1)}, u32[]{:S(2)}, u32[]{:S(2)}) collective-permute-start(bf16[2320,128]{1,0:T(8,128)(2,1)S(1)} %get-tuple-element.10.right_0), channel_id=1, source_target_pairs={{0,928},{1,929},{2,930},{3,931},{4,932},{5,933},{6,934},{7,935},{8... | collective-permute-start | bytes 1781768 | tf_op jit(solution)/shard_map/ppermute | solution.py:170
  33.1 3.5 %collective-permute-start.2 = (bf16[2320,128]{1,0:T(8,128)(2,1)S(1)}, bf16[2320,128]{1,0:T(8,128)(2,1)}, u32[]{:S(2)}, u32[]{:S(2)}) collective-permute-start(bf16[2320,128]{1,0:T(8,128)(2,1)S(1)} %get-tuple-element.9.left_0), channel_id=1, source_target_pairs={{0,29},{1,30},{2,31},{3,0},{4,1},{5,2},{6,3},{7,4},{8,5},{9,6},{10... | collective-permute-start | bytes 1781768 | tf_op jit(solution)/shard_map/ppermute | solution.py:170
  36.7 15.0 %collective-permute-done.3.right_3 = bf16[2320,128]{1,0:T(8,128)(2,1)S(1)} collective-permute-done((bf16[2320,128]{1,0:T(8,128)(2,1)S(1)}, bf16[2320,128]{1,0:T(8,128)(2,1)S(1)}, u32[]{:S(2)}, u32[]{:S(2)}) %collective-permute-start.3) | collective-permute-done | bytes 593952 | tf_op jit(solution)/shard_map/ppermute | solution.py:170
  51.7 6.8 %collective-permute-start.4 = (bf16[2320,128]{1,0:T(8,128)(2,1)S(1)}, bf16[2320,128]{1,0:T(8,128)(2,1)}, u32[]{:S(2)}, u32[]{:S(2)}) collective-permute-start(bf16[2320,128]{1,0:T(8,128)(2,1)S(1)} %collective-permute-done.3.right_3), channel_id=1, source_target_pairs={{0,32},{1,33},{2,34},{3,35},{4,36},{5,37},{6,38},{7,39},{8,40},{9,... | collective-permute-start | bytes 1781768 | tf_op jit(solution)/shard_map/ppermute | solution.py:170
  58.5 2.9 %collective-permute-done.left_1 = bf16[2320,128]{1,0:T(8,128)(2,1)S(1)} collective-permute-done((bf16[2320,128]{1,0:T(8,128)(2,1)S(1)}, bf16[2320,128]{1,0:T(8,128)(2,1)S(1)}, u32[]{:S(2)}, u32[]{:S(2)}) %collective-permute-start) | collective-permute-done | bytes 593952 | tf_op jit(solution)/shard_map/ppermute | solution.py:170
  61.4 7.9 %collective-permute-start.5 = (bf16[2320,128]{1,0:T(8,128)(2,1)S(1)}, bf16[2320,128]{1,0:T(8,128)(2,1)S(1)}, u32[]{:S(2)}, u32[]{:S(2)}) collective-permute-start(bf16[2320,128]{1,0:T(8,128)(2,1)S(1)} %collective-permute-done.left_1), channel_id=1, source_target_pairs={{0,31},{1,0},{2,1},{3,2},{4,3},{5,4},{6,5},{7,6},{8,7},{9,8},{10,9... | collective-permute-start | bytes 1781768 | tf_op jit(solution)/shard_map/ppermute | solution.py:170
  69.3 0.0 collective-permute-done.1.right_1
  69.4 0.0 collective-permute-done.2.left_2
  69.4 0.0 collective-permute-done.4.right_2
  69.4 6.6 %first_three_products.1 = (f32[768,768]{1,0:T(8,128)S(1)}, bf16[896,768]{1,0:T(8,128)(2,1)S(1)}) custom-call(bf16[2320,128]{1,0:T(8,128)(2,1)S(1)} %get-tuple-element.9.left_0, bf16[2320,128]{1,0:T(8,128)(2,1)S(1)} %get-tuple-element.10.right_0, bf16[2320,128]{1,0:T(8,128)(2,1)S(1)} %collective-permute-done.left_1, ...), custom_call_target="tpu_custom_call" | custom-call | flops 2717908992 | bytes 10000000 | tf_op jit(solution)/shard_map/first_three_products/pallas_call | solution.py:133
  75.9 0.3 collective-permute-done.5.left_3
  76.3 2.9 %last_product.1 = (bf16[768,768]{1,0:T(8,128)(2,1)}, f32[32,128]{1,0:T(8,128)S(1)}) custom-call(s32[1]{0:T(128)} %bitcast.on_diagonal, f32[768,768]{1,0:T(8,128)S(1)} %get-tuple-element.11.accum, bf16[896,768]{1,0:T(8,128)(2,1)S(1)} %get-tuple-element.12.right_dense, bf16[2320,128]{1,0:T(8,128)(2,1)S(1)} %collective-permute-done.5.left_3), custom_call_target="tpu_custom_call" | custom-call | flops 905969664 | bytes 6000000 | tf_op jit(solution)/shard_map/last_product/pallas_call | solution.py:149
  79.2 20.7 %all_to_all.15 = f32[32,1,128]{2,1,0:T(1,128)S(1)} all-to-all(f32[32,1,128]{2,1,0:T(1,128)S(1)} %bitcast.11), channel_id=1, replica_groups=mesh['row'=32,'col'=32] {'row'}, dimensions={0} | all-to-all | bytes 32768 | tf_op jit(solution)/shard_map/all_to_all | solution.py:174
  100.0 0.1 reduce_sum.18
  100.0 18.9 %all_to_all.16 = f32[32,1,128]{2,1,0:T(1,128)S(1)} all-to-all(f32[32,1,128]{2,1,0:T(1,128)S(1)} %broadcast_in_dim.2), channel_id=1, replica_groups=mesh['row'=32,'col'=32] {'col'}, dimensions={0} | all-to-all | bytes 32768 | tf_op jit(solution)/shard_map/all_to_all | solution.py:174
  119.0 0.6 fusion
  (2 shorter events, 0.0 us)
Async XLA Ops:
  0.6 1.1 copy-start
  1.7 1.1 copy-start.1
  2.8 0.7 copy-start.2
  3.4 0.7 copy-start.3
  4.9 46.8 %collective-permute-start.3 = (bf16[2320,128]{1,0:T(8,128)(2,1)S(1)}, bf16[2320,128]{1,0:T(8,128)(2,1)S(1)}, u32[]{:S(2)}, u32[]{:S(2)}) collective-permute-start(bf16[2320,128]{1,0:T(8,128)(2,1)S(1)} %get-tuple-element.10.right_0), channel_id=1, source_target_pairs={{0,960},{1,961},{2,962},{3,963},{4,964},{5,965},{6,966},{7,967},{8... | collective-permute-start | bytes 1781768 | tf_op jit(solution)/shard_map/ppermute | solution.py:170
  23.9 37.5 %collective-permute-start = (bf16[2320,128]{1,0:T(8,128)(2,1)S(1)}, bf16[2320,128]{1,0:T(8,128)(2,1)S(1)}, u32[]{:S(2)}, u32[]{:S(2)}) collective-permute-start(bf16[2320,128]{1,0:T(8,128)(2,1)S(1)} %get-tuple-element.9.left_0), channel_id=1, source_target_pairs={{0,31},{1,0},{2,1},{3,2},{4,3},{5,4},{6,5},{7,6},{8,7},{9,8},{10,9... | collective-permute-start | bytes 1781768 | tf_op jit(solution)/shard_map/ppermute | solution.py:170
  30.7 38.7 %collective-permute-start.1 = (bf16[2320,128]{1,0:T(8,128)(2,1)S(1)}, bf16[2320,128]{1,0:T(8,128)(2,1)}, u32[]{:S(2)}, u32[]{:S(2)}) collective-permute-start(bf16[2320,128]{1,0:T(8,128)(2,1)S(1)} %get-tuple-element.10.right_0), channel_id=1, source_target_pairs={{0,928},{1,929},{2,930},{3,931},{4,932},{5,933},{6,934},{7,935},{8... | collective-permute-start | bytes 1781768 | tf_op jit(solution)/shard_map/ppermute | solution.py:170
  33.1 36.2 %collective-permute-start.2 = (bf16[2320,128]{1,0:T(8,128)(2,1)S(1)}, bf16[2320,128]{1,0:T(8,128)(2,1)}, u32[]{:S(2)}, u32[]{:S(2)}) collective-permute-start(bf16[2320,128]{1,0:T(8,128)(2,1)S(1)} %get-tuple-element.9.left_0), channel_id=1, source_target_pairs={{0,29},{1,30},{2,31},{3,0},{4,1},{5,2},{6,3},{7,4},{8,5},{9,6},{10... | collective-permute-start | bytes 1781768 | tf_op jit(solution)/shard_map/ppermute | solution.py:170
  51.7 17.6 %collective-permute-start.4 = (bf16[2320,128]{1,0:T(8,128)(2,1)S(1)}, bf16[2320,128]{1,0:T(8,128)(2,1)}, u32[]{:S(2)}, u32[]{:S(2)}) collective-permute-start(bf16[2320,128]{1,0:T(8,128)(2,1)S(1)} %collective-permute-done.3.right_3), channel_id=1, source_target_pairs={{0,32},{1,33},{2,34},{3,35},{4,36},{5,37},{6,38},{7,39},{8,40},{9,... | collective-permute-start | bytes 1781768 | tf_op jit(solution)/shard_map/ppermute | solution.py:170
  61.4 14.9 %collective-permute-start.5 = (bf16[2320,128]{1,0:T(8,128)(2,1)S(1)}, bf16[2320,128]{1,0:T(8,128)(2,1)S(1)}, u32[]{:S(2)}, u32[]{:S(2)}) collective-permute-start(bf16[2320,128]{1,0:T(8,128)(2,1)S(1)} %collective-permute-done.left_1), channel_id=1, source_target_pairs={{0,31},{1,0},{2,1},{3,2},{4,3},{5,4},{6,5},{7,6},{8,7},{9,8},{10,9... | collective-permute-start | bytes 1781768 | tf_op jit(solution)/shard_map/ppermute | solution.py:170

commit v4 on v3

v4 whole, which is shorter than its diff:
```python
import functools
import math

import jax
import jax.numpy as jnp
from jax import lax
from jax.experimental import pallas as pl
from jax.experimental.pallas import tpu as pltpu
from jax.sharding import PartitionSpec as P

BLK = 128
TB = 6
STEPS = 4
TILE = TB * BLK
WIDTH = 2 * BLK
TAIL = 16
LANES = 128
BOTH = ("row", "col")


def pack_kernel(left_slots, right_slots, left, right, left_out, right_out, held, read_sems, write_sems, tail_sems):
    depth = left.shape[0]
    part = depth // PARTS
    sides = ((right_slots, right, right_out), (left_slots, left, left_out))
    reads = []
    for side, (_, source, _) in enumerate(sides):
        for index in range(PARTS):
            rows = pl.ds(index * part, part)
            reads.append(pltpu.make_async_copy(source.at[rows], held.at[side, rows], read_sems.at[side, index]))
            reads[-1].start()
    lane = lax.broadcasted_iota(jnp.int32, (TAIL, LANES), 1)
    tail = pl.ds(depth, TAIL)
    writes = []
    for side, (slots, _, out) in enumerate(sides):
        cells = jnp.zeros((TAIL, LANES), jnp.int32)
        for slot in range(slots.shape[1]):
            cells = jnp.where(lane == slot, slots[0, slot], cells)
        held[side, depth : depth + TAIL, :] = cells.astype(jnp.float32).astype(out.dtype)
        writes.append(pltpu.make_async_copy(held.at[side, tail], out.at[tail], tail_sems.at[side]))
        writes[-1].start()
    for side, (_, _, out) in enumerate(sides):
        for index in range(PARTS):
            rows = pl.ds(index * part, part)
            reads[side * PARTS + index].wait()
            writes.append(pltpu.make_async_copy(held.at[side, rows], out.at[rows], write_sems.at[side, index]))
            writes[-1].start()
    for copy in writes:
        copy.wait()


PARTS = 3


def pack(left_slots, right_slots, left, right):
    depth = left.shape[0]
    packed = jax.ShapeDtypeStruct((depth + TAIL, LANES), left.dtype)
    return pl.pallas_call(
        pack_kernel,
        out_shape=(packed, packed),
        in_specs=[pl.BlockSpec(memory_space=pltpu.SMEM)] * 2 + [pl.BlockSpec(memory_space=pl.ANY)] * 2,
        out_specs=(pl.BlockSpec(memory_space=pl.ANY),) * 2,
        scratch_shapes=[
            pltpu.VMEM((2, depth + TAIL, LANES), left.dtype),
            pltpu.SemaphoreType.DMA((2, PARTS)),
            pltpu.SemaphoreType.DMA((2, PARTS)),
            pltpu.SemaphoreType.DMA((2,)),
        ],
        name="pack_tiles",
    )(left_slots, right_slots, left, right)


def gather_cells(tiles, cells, table, sem):
    depth = tiles[0].shape[0] - TAIL
    level = lax.broadcasted_iota(jnp.int32, cells.shape, 0)
    gathered = jnp.zeros(cells.shape, jnp.int32)
    for index, tile in enumerate(tiles):
        tail = tile[depth : depth + TAIL, :].astype(jnp.float32).astype(jnp.int32)
        gathered = jnp.where(level == index, tail[0 : cells.shape[0]], gathered)
    cells[...] = gathered
    copy = pltpu.make_async_copy(cells, table, sem)
    copy.start()
    return copy


def place(tile, table, index, dense, base, side):
    for slot in range((tile.shape[0] - TAIL) // BLK):
        cell = table[index, slot]
        row, col = cell // TB * BLK, cell % TB * BLK
        if side == "left":
            col = base + col
        else:
            row = jnp.where(cell < TB * TB, base + row, dense.shape[0] - BLK)
        row, col = pl.multiple_of(row, BLK), pl.multiple_of(col, BLK)
        dense[pl.ds(row, BLK), pl.ds(col, BLK)] = tile[slot * BLK : (slot + 1) * BLK, :]


def early_kernel(*refs):
    tiles, (accum, left_dense, right_dense, cells, table, sem) = refs[: 2 * EARLY], refs[2 * EARLY :]
    place_pairs(tiles, left_dense, right_dense, cells, table, sem)
    for low in range(0, TILE, WIDTH):
        accum[:, low : low + WIDTH] = multiply_pairs(left_dense, right_dense, low)


def late_kernel(on_diagonal, accum, *refs):
    tiles, rest = refs[: 2 * LATE], refs[2 * LATE :]
    out, sums, left_dense, right_dense, cells, table, sem, rounded, out_sems = rest
    place_pairs(tiles, left_dense, right_dense, cells, table, sem)
    inside = lax.broadcasted_iota(jnp.int32, (BLK, BLK), 0) == lax.broadcasted_iota(jnp.int32, (BLK, BLK), 1)
    squares = jnp.zeros((8, WIDTH), jnp.float32)
    diagonal = jnp.zeros((8, BLK), jnp.float32)
    copies = []
    for part in range(TILE // WIDTH):
        low = part * WIDTH
        columns = pl.ds(low, WIDTH)
        total = accum[:, low : low + WIDTH] + multiply_pairs(left_dense, right_dense, low)
        rounded[:, low : low + WIDTH] = total.astype(rounded.dtype)
        copies.append(pltpu.make_async_copy(rounded.at[:, columns], out.at[:, columns], out_sems.at[part]))
        copies[-1].start()
        squares += jnp.sum((total * total).reshape(-1, 8, WIDTH), axis=0)
        for block in range(0, WIDTH, BLK):
            corner = total[low + block : low + block + BLK, block : block + BLK]
            diagonal += jnp.sum(jnp.where(inside, corner, 0.0).reshape(-1, 8, BLK), axis=0)
    diagonal_sum = jnp.where(on_diagonal[0] > 0, jnp.sum(diagonal), 0.0)
    lane = lax.broadcasted_iota(jnp.int32, sums.shape, 1)
    sums[...] = jnp.where(lane == 0, diagonal_sum, jnp.where(lane == 1, jnp.sum(squares), 0.0))
    for copy in copies:
        copy.wait()


def place_pairs(tiles, left_dense, right_dense, cells, table, sem):
    copy = gather_cells(tiles, cells, table, sem)
    left_dense[...] = jnp.zeros_like(left_dense)
    right_dense[...] = jnp.zeros_like(right_dense)
    copy.wait()
    for step in range(len(tiles) // 2):
        place(tiles[2 * step], table, 2 * step, left_dense, step * TILE, "left")
        place(tiles[2 * step + 1], table, 2 * step + 1, right_dense, step * TILE, "right")


def multiply_pairs(left_dense, right_dense, low):
    depth = left_dense.shape[1]
    return jnp.dot(
        left_dense[0:TILE, :],
        right_dense[0:depth, low : low + WIDTH],
        preferred_element_type=jnp.float32,
    )


WHOLE = pl.BlockSpec(memory_space=pltpu.VMEM)
EARLY = 2
LATE = STEPS - EARLY
CELLS = [pltpu.VMEM((8, LANES), jnp.int32), pltpu.SMEM((8, LANES), jnp.int32), pltpu.SemaphoreType.DMA]


def left_shape(steps):
    return (TILE + BLK, steps * TILE)


def right_shape(steps):
    return (steps * TILE + BLK, TILE)


def scratch(steps):
    return [pltpu.VMEM(left_shape(steps), jnp.bfloat16), pltpu.VMEM(right_shape(steps), jnp.bfloat16)] + CELLS


def multiply_early(tiles):
    return pl.pallas_call(
        early_kernel,
        out_shape=jax.ShapeDtypeStruct((TILE, TILE), jnp.float32),
        in_specs=[WHOLE] * len(tiles),
        out_specs=WHOLE,
        scratch_shapes=scratch(EARLY),
        compiler_params=pltpu.CompilerParams(vmem_limit_bytes=24 * 2**20),
        cost_estimate=pl.CostEstimate(flops=2 * EARLY * TILE**3, bytes_accessed=5_000_000, transcendentals=0),
        name="early_products",
    )(*tiles)


def multiply_late(on_diagonal, accum, tiles, fan):
    return pl.pallas_call(
        late_kernel,
        out_shape=(
            jax.ShapeDtypeStruct((TILE, TILE), jnp.bfloat16),
            jax.ShapeDtypeStruct((fan, LANES), jnp.float32),
        ),
        in_specs=[pl.BlockSpec(memory_space=pltpu.SMEM)] + [WHOLE] * (1 + len(tiles)),
        out_specs=(pl.BlockSpec(memory_space=pl.ANY), WHOLE),
        scratch_shapes=scratch(LATE)
        + [pltpu.VMEM((TILE, TILE), jnp.bfloat16), pltpu.SemaphoreType.DMA((TILE // WIDTH,))],
        compiler_params=pltpu.CompilerParams(vmem_limit_bytes=24 * 2**20),
        cost_estimate=pl.CostEstimate(flops=2 * LATE * TILE**3, bytes_accessed=6_000_000, transcendentals=0),
        name="late_products",
    )(on_diagonal, accum, *tiles)


def exchange(value, target, rows, cols):
    pairs = []
    for i in range(rows):
        for j in range(cols):
            to_row, to_col = target(i, j)
            pairs.append((i * cols + j, to_row % rows * cols + to_col % cols))
    return lax.ppermute(value, BOTH, pairs)


def spread_sum(values, axis):
    return lax.all_to_all(values, axis, 0, 0, tiled=True)


def body(left_blocks, left_slots, right_blocks, right_slots):
    rows, cols = lax.axis_size("row"), lax.axis_size("col")
    on_diagonal = (lax.axis_index("row") == lax.axis_index("col")).astype(jnp.int32).reshape(1)
    left, right = pack(
        left_slots, right_slots, left_blocks.reshape(-1, LANES), right_blocks.reshape(-1, LANES)
    )
    move = functools.partial(exchange, rows=rows, cols=cols)
    left_first = move(left, lambda i, j: (i, j - 1 if i % 2 == 0 else j - 3))
    right_middle = move(right, lambda i, j: (i - 2, j))
    left_second = move(left, lambda i, j: (i, j - 3 if i % 2 == 0 else j - 1))
    right_first = move(right, lambda i, j: (i - 1 if i % 2 else i - 3, j))
    left_middle = move(left_first, lambda i, j: (i, j - 1 if i % 2 == 0 else j + 1))
    right_second = move(right_middle, lambda i, j: (i ^ 1, j))
    accum = multiply_early((left, right, left_first, right_first))
    late = (left_middle, right_middle, left_second, right_second)
    product, partial = multiply_late(on_diagonal, accum, late, rows)
    row_sums = jnp.sum(spread_sum(partial, "row"), axis=0, keepdims=True)
    totals = jnp.sum(spread_sum(jnp.broadcast_to(row_sums, (cols, LANES)), "col"), axis=0)
    trace_scaled = totals[0] / math.sqrt(min(rows, cols) * TILE)
    norm_scaled = totals[1] / (rows * cols * TILE * TILE)
    return product, trace_scaled, norm_scaled


def solution(mesh):
    placed = (
        P("row", "col", None, None),
        P("row", "col"),
        P("row", "col", None, None),
        P("row", "col"),
    )
    return jax.shard_map(
        body, mesh=mesh, in_specs=placed, out_specs=(P("row", "col"), P(), P()), check_vma=False
    )
```

time: 124 us -> 125 us (level)
  waiting for transfers between devices: 18.3 us -> 23.9 us
  starting transfers between devices: 46.4 us -> 41.2 us
  Pallas kernels: 10.3 us -> 11.8 us
  local copies, waits for them, and re-layouts: 4.03 us -> 2.73 us
    ppermute x6, waiting for transfers between devices: 18.3 us -> 23.9 us  [exchange(): return lax.ppermute(value, BOTH, pairs)]
    ppermute x6, starting transfers between devices: 46.4 us -> 41.2 us  [exchange(): return lax.ppermute(value, BOTH, pairs)]
    pallas_call x1, Pallas kernels: 6.55 us -> 3.5 us  [multiply_early(): pl.pallas_call(early_kernel, out_shape=jax.ShapeDtypeStruct((TILE, TILE),...]
    pallas_call x1, Pallas kernels: 2.94 us -> 5.52 us  [multiply_late(): pl.pallas_call(late_kernel, out_shape=(jax.ShapeDtypeStruct((TILE, TILE),...]
    pallas_call x1, Pallas kernels: 0.82 us -> 2.82 us  [pack(): pl.pallas_call(pack_kernel, out_shape=(packed, packed), in_specs=[pl.Bloc...]
    unnamed x8 -> x4, local copies, waits for them, and re-layouts: 3.43 us -> 2.13 us
  transfers between devices with their start and end apart: 6 -> 6, of which waited for: 3 -> 1; matrix products, arithmetic and copies ran while one was open for 0% -> 0% of each run, Pallas kernels for 5% -> 3%
where the time goes in v4:
time: 125 us; the launch traced here: 124 us
  starting transfers between devices  41.2 us (33%)
  blocking collectives  39.9 us (32%)
  waiting for transfers between devices  23.9 us (19%)
  Pallas kernels  11.8 us (9%)
  between operations  4.31 us (3%)
  local copies, waits for them, and re-layouts  2.73 us (2%)
    ppermute x6, starting transfers between devices, exchange(): return lax.ppermute(value, BOTH, pairs)  41.2 us
    all_to_all x2, blocking collectives, spread_sum(): return lax.all_to_all(values, axis, 0, 0, tiled=True)  39.9 us
    ppermute x6, waiting for transfers between devices, exchange(): return lax.ppermute(value, BOTH, pairs)  23.9 us
    pallas_call x1, Pallas kernels, multiply_late(): pl.pallas_call(late_kernel, out_shape=(jax.ShapeDtypeStruct((TILE, TILE),...  5.52 us
    pallas_call x1, Pallas kernels, multiply_early(): pl.pallas_call(early_kernel, out_shape=jax.ShapeDtypeStruct((TILE, TILE),...  3.5 us
    pallas_call x1, Pallas kernels, pack(): pl.pallas_call(pack_kernel, out_shape=(packed, packed), in_specs=[pl.Bloc...  2.82 us
  transfers between devices with their start and end apart: 6, of which 1 were waited for; matrix products, arithmetic and copies ran while one was open for 0% of the time, Pallas kernels for 3%

profile of v4, /device:TPU:1, one launch (start us, length us, event | category | flops | bytes accessed | tf_op | source)
XLA Modules:
  0.0 124.0 jit_solution(14960842472777154343)
XLA Ops:
  0.6 2.8 %pack_tiles.1 = (bf16[2320,128]{1,0:T(8,128)(2,1)}, bf16[2320,128]{1,0:T(8,128)(2,1)}) custom-call(s32[1,18]{1,0:T(1,128)} %left_slots.1, s32[1,18]{1,0:T(1,128)} %right_slots.1, bf16[2304,128]{1,0:T(8,128)(2,1)} %bitcast.10, bf16[2304,128]{1,0:T(8,128)(2,1)} %bitcast.11), custom_call_target="tpu_custom_call" | custom-call | tf_op jit(solution)/shard_map/pack_tiles/pallas_call | solution.py:57
  3.5 7.6 %collective-permute-start = (bf16[2320,128]{1,0:T(8,128)(2,1)}, bf16[2320,128]{1,0:T(8,128)(2,1)S(1)}, u32[]{:S(2)}, u32[]{:S(2)}) collective-permute-start(bf16[2320,128]{1,0:T(8,128)(2,1)} %get-tuple-element.7.refs_0_), channel_id=1, source_target_pairs={{0,31},{1,0},{2,1},{3,2},{4,3},{5,4},{6,5},{7,6},{8,7},{9,8},{10,9... | collective-permute-start | bytes 1781768 | tf_op jit(solution)/shard_map/ppermute | solution.py:203
  11.1 18.7 %collective-permute-start.3 = (bf16[2320,128]{1,0:T(8,128)(2,1)}, bf16[2320,128]{1,0:T(8,128)(2,1)S(1)}, u32[]{:S(2)}, u32[]{:S(2)}) collective-permute-start(bf16[2320,128]{1,0:T(8,128)(2,1)} %get-tuple-element.8.refs_1_), channel_id=1, source_target_pairs={{0,960},{1,961},{2,962},{3,963},{4,964},{5,965},{6,966},{7,967},{8... | collective-permute-start | bytes 1781768 | tf_op jit(solution)/shard_map/ppermute | solution.py:203
  29.8 2.0 %collective-permute-start.1 = (bf16[2320,128]{1,0:T(8,128)(2,1)}, bf16[2320,128]{1,0:T(8,128)(2,1)S(1)}, u32[]{:S(2)}, u32[]{:S(2)}) collective-permute-start(bf16[2320,128]{1,0:T(8,128)(2,1)} %get-tuple-element.8.refs_1_), channel_id=1, source_target_pairs={{0,928},{1,929},{2,930},{3,931},{4,932},{5,933},{6,934},{7,935},{8... | collective-permute-start | bytes 1781768 | tf_op jit(solution)/shard_map/ppermute | solution.py:203
  31.7 3.5 %collective-permute-start.4 = (bf16[2320,128]{1,0:T(8,128)(2,1)}, bf16[2320,128]{1,0:T(8,128)(2,1)S(1)}, u32[]{:S(2)}, u32[]{:S(2)}) collective-permute-start(bf16[2320,128]{1,0:T(8,128)(2,1)} %get-tuple-element.7.refs_0_), channel_id=1, source_target_pairs={{0,29},{1,30},{2,31},{3,0},{4,1},{5,2},{6,3},{7,4},{8,5},{9,6},{10... | collective-permute-start | bytes 1781768 | tf_op jit(solution)/shard_map/ppermute | solution.py:203
  35.2 0.0 collective-permute-done.refs_2_
  35.3 2.7 %collective-permute-start.2 = (bf16[2320,128]{1,0:T(8,128)(2,1)S(1)}, bf16[2320,128]{1,0:T(8,128)(2,1)S(1)}, u32[]{:S(2)}, u32[]{:S(2)}) collective-permute-start(bf16[2320,128]{1,0:T(8,128)(2,1)S(1)} %collective-permute-done.refs_2_), channel_id=1, source_target_pairs={{0,31},{1,0},{2,1},{3,2},{4,3},{5,4},{6,5},{7,6},{8,7},{9,8},{10,9... | collective-permute-start | bytes 1781768 | tf_op jit(solution)/shard_map/ppermute | solution.py:203
  37.9 23.9 %collective-permute-done.3.refs_1_ = bf16[2320,128]{1,0:T(8,128)(2,1)S(1)} collective-permute-done((bf16[2320,128]{1,0:T(8,128)(2,1)}, bf16[2320,128]{1,0:T(8,128)(2,1)S(1)}, u32[]{:S(2)}, u32[]{:S(2)}) %collective-permute-start.3) | collective-permute-done | bytes 593952 | tf_op jit(solution)/shard_map/ppermute | solution.py:203
  61.9 6.8 %collective-permute-start.5 = (bf16[2320,128]{1,0:T(8,128)(2,1)S(1)}, bf16[2320,128]{1,0:T(8,128)(2,1)}, u32[]{:S(2)}, u32[]{:S(2)}) collective-permute-start(bf16[2320,128]{1,0:T(8,128)(2,1)S(1)} %collective-permute-done.3.refs_1_), channel_id=1, source_target_pairs={{0,32},{1,33},{2,34},{3,35},{4,36},{5,37},{6,38},{7,39},{8,40},{9,... | collective-permute-start | bytes 1781768 | tf_op jit(solution)/shard_map/ppermute | solution.py:203
  68.6 0.0 collective-permute-done.1.refs_3_
  68.6 0.0 copy-start
  68.7 1.1 copy-done
  69.7 0.0 copy-start.1
  69.7 1.1 copy-done.1
  70.8 3.5 %early_products.1.accum = f32[768,768]{1,0:T(8,128)S(1)} custom-call(bf16[2320,128]{1,0:T(8,128)(2,1)S(1)} %copy-done, bf16[2320,128]{1,0:T(8,128)(2,1)S(1)} %copy-done.1, bf16[2320,128]{1,0:T(8,128)(2,1)S(1)} %collective-permute-done.refs_2_, bf16[2320,128]{1,0:T(8,128)(2,1)S(1)} %collective-permute-done.1.refs_3_), custom_call_target="tpu_custom_call" | custom-call | flops 1811939328 | bytes 5000000 | tf_op jit(solution)/shard_map/early_products/pallas_call | solution.py:168
  74.3 0.0 collective-permute-done.4.refs_2_
  74.3 0.0 collective-permute-done.2.refs_0_
  74.3 0.0 collective-permute-done.5.refs_3_
  74.3 5.5 %late_products.1 = (bf16[768,768]{1,0:T(8,128)(2,1)}, f32[32,128]{1,0:T(8,128)S(1)}) custom-call(s32[1]{0:T(128)} %bitcast.on_diagonal, f32[768,768]{1,0:T(8,128)S(1)} %early_products.1.accum, bf16[2320,128]{1,0:T(8,128)(2,1)S(1)} %collective-permute-done.2.refs_0_, bf16[2320,128]{1,0:T(8,128)(2,1)S(1)} %collective-permute-done.3.refs_1_, ...), custom_call_target="tpu_custom_call" | custom-call | flops 1811939328 | bytes 6000000 | tf_op jit(solution)/shard_map/late_products/pallas_call | solution.py:181
  79.8 23.1 %all_to_all.15 = f32[32,1,128]{2,1,0:T(1,128)S(1)} all-to-all(f32[32,1,128]{2,1,0:T(1,128)S(1)} %bitcast.9), channel_id=1, replica_groups=mesh['row'=32,'col'=32] {'row'}, dimensions={0} | all-to-all | bytes 32768 | tf_op jit(solution)/shard_map/all_to_all | solution.py:207
  103.0 0.1 reduce_sum.18
  103.1 16.8 %all_to_all.16 = f32[32,1,128]{2,1,0:T(1,128)S(1)} all-to-all(f32[32,1,128]{2,1,0:T(1,128)S(1)} %broadcast_in_dim.2), channel_id=1, replica_groups=mesh['row'=32,'col'=32] {'col'}, dimensions={0} | all-to-all | bytes 32768 | tf_op jit(solution)/shard_map/all_to_all | solution.py:207
  119.8 0.6 fusion
  (2 shorter events, 0.0 us)
Async XLA Ops:
  3.5 31.8 %collective-permute-start = (bf16[2320,128]{1,0:T(8,128)(2,1)}, bf16[2320,128]{1,0:T(8,128)(2,1)S(1)}, u32[]{:S(2)}, u32[]{:S(2)}) collective-permute-start(bf16[2320,128]{1,0:T(8,128)(2,1)} %get-tuple-element.7.refs_0_), channel_id=1, source_target_pairs={{0,31},{1,0},{2,1},{3,2},{4,3},{5,4},{6,5},{7,6},{8,7},{9,8},{10,9... | collective-permute-start | bytes 1781768 | tf_op jit(solution)/shard_map/ppermute | solution.py:203
  11.1 50.8 %collective-permute-start.3 = (bf16[2320,128]{1,0:T(8,128)(2,1)}, bf16[2320,128]{1,0:T(8,128)(2,1)S(1)}, u32[]{:S(2)}, u32[]{:S(2)}) collective-permute-start(bf16[2320,128]{1,0:T(8,128)(2,1)} %get-tuple-element.8.refs_1_), channel_id=1, source_target_pairs={{0,960},{1,961},{2,962},{3,963},{4,964},{5,965},{6,966},{7,967},{8... | collective-permute-start | bytes 1781768 | tf_op jit(solution)/shard_map/ppermute | solution.py:203
  29.8 38.9 %collective-permute-start.1 = (bf16[2320,128]{1,0:T(8,128)(2,1)}, bf16[2320,128]{1,0:T(8,128)(2,1)S(1)}, u32[]{:S(2)}, u32[]{:S(2)}) collective-permute-start(bf16[2320,128]{1,0:T(8,128)(2,1)} %get-tuple-element.8.refs_1_), channel_id=1, source_target_pairs={{0,928},{1,929},{2,930},{3,931},{4,932},{5,933},{6,934},{7,935},{8... | collective-permute-start | bytes 1781768 | tf_op jit(solution)/shard_map/ppermute | solution.py:203
  31.7 42.5 %collective-permute-start.4 = (bf16[2320,128]{1,0:T(8,128)(2,1)}, bf16[2320,128]{1,0:T(8,128)(2,1)S(1)}, u32[]{:S(2)}, u32[]{:S(2)}) collective-permute-start(bf16[2320,128]{1,0:T(8,128)(2,1)} %get-tuple-element.7.refs_0_), channel_id=1, source_target_pairs={{0,29},{1,30},{2,31},{3,0},{4,1},{5,2},{6,3},{7,4},{8,5},{9,6},{10... | collective-permute-start | bytes 1781768 | tf_op jit(solution)/shard_map/ppermute | solution.py:203
  35.3 39.0 %collective-permute-start.2 = (bf16[2320,128]{1,0:T(8,128)(2,1)S(1)}, bf16[2320,128]{1,0:T(8,128)(2,1)S(1)}, u32[]{:S(2)}, u32[]{:S(2)}) collective-permute-start(bf16[2320,128]{1,0:T(8,128)(2,1)S(1)} %collective-permute-done.refs_2_), channel_id=1, source_target_pairs={{0,31},{1,0},{2,1},{3,2},{4,3},{5,4},{6,5},{7,6},{8,7},{9,8},{10,9... | collective-permute-start | bytes 1781768 | tf_op jit(solution)/shard_map/ppermute | solution.py:203
  61.9 12.5 %collective-permute-start.5 = (bf16[2320,128]{1,0:T(8,128)(2,1)S(1)}, bf16[2320,128]{1,0:T(8,128)(2,1)}, u32[]{:S(2)}, u32[]{:S(2)}) collective-permute-start(bf16[2320,128]{1,0:T(8,128)(2,1)S(1)} %collective-permute-done.3.refs_1_), channel_id=1, source_target_pairs={{0,32},{1,33},{2,34},{3,35},{4,36},{5,37},{6,38},{7,39},{8,40},{9,... | collective-permute-start | bytes 1781768 | tf_op jit(solution)/shard_map/ppermute | solution.py:203
  68.6 1.1 copy-start
  69.7 1.1 copy-start.1

commit v5 on v4

--- a/solution.py
+++ b/solution.py
@@ -18,10 +18,14 @@
 BOTH = ("row", "col")
 
 
-def pack_kernel(left_slots, right_slots, left, right, left_out, right_out, held, read_sems, write_sems, tail_sems):
+def pack_kernel(left_slots, right_slots, left, right, left_out, right_out, held, table, read_sems, write_sems, tail_sems, slot_sems):
     depth = left.shape[0]
     part = depth // PARTS
-    sides = ((right_slots, right, right_out), (left_slots, left, left_out))
+    sides = ((left_slots, left, left_out), (right_slots, right, right_out))
+    fetches = []
+    for side, (slots, _, _) in enumerate(sides):
+        fetches.append(pltpu.make_async_copy(slots, table.at[side], slot_sems.at[side]))
+        fetches[-1].start()
     reads = []
     for side, (_, source, _) in enumerate(sides):
         for index in range(PARTS):
@@ -32,9 +36,10 @@
     tail = pl.ds(depth, TAIL)
     writes = []
     for side, (slots, _, out) in enumerate(sides):
+        fetches[side].wait()
         cells = jnp.zeros((TAIL, LANES), jnp.int32)
         for slot in range(slots.shape[1]):
-            cells = jnp.where(lane == slot, slots[0, slot], cells)
+            cells = jnp.where(lane == slot, table[side, 0, slot], cells)
         held[side, depth : depth + TAIL, :] = cells.astype(jnp.float32).astype(out.dtype)
         writes.append(pltpu.make_async_copy(held.at[side, tail], out.at[tail], tail_sems.at[side]))
         writes[-1].start()
@@ -57,12 +62,14 @@
     return pl.pallas_call(
         pack_kernel,
         out_shape=(packed, packed),
-        in_specs=[pl.BlockSpec(memory_space=pltpu.SMEM)] * 2 + [pl.BlockSpec(memory_space=pl.ANY)] * 2,
+        in_specs=[pl.BlockSpec(memory_space=pl.ANY)] * 4,
         out_specs=(pl.BlockSpec(memory_space=pl.ANY),) * 2,
         scratch_shapes=[
             pltpu.VMEM((2, depth + TAIL, LANES), left.dtype),
+            pltpu.SMEM((2,) + left_slots.shape, jnp.int32),
             pltpu.SemaphoreType.DMA((2, PARTS)),
             pltpu.SemaphoreType.DMA((2, PARTS)),
+            pltpu.SemaphoreType.DMA((2,)),
             pltpu.SemaphoreType.DMA((2,)),
         ],
         name="pack_tiles",
@@ -94,17 +101,23 @@
         dense[pl.ds(row, BLK), pl.ds(col, BLK)] = tile[slot * BLK : (slot + 1) * BLK, :]
 
 
-def early_kernel(*refs):
-    tiles, (accum, left_dense, right_dense, cells, table, sem) = refs[: 2 * EARLY], refs[2 * EARLY :]
-    place_pairs(tiles, left_dense, right_dense, cells, table, sem)
+def first_kernel(left_0, right_0, left_1, right_1, accum, *scratches):
+    left_dense, right_dense, cells, table, sem = scratches
+    place_pairs((left_0, right_0, left_1, right_1), left_dense, right_dense, cells, table, sem)
     for low in range(0, TILE, WIDTH):
         accum[:, low : low + WIDTH] = multiply_pairs(left_dense, right_dense, low)
 
 
-def late_kernel(on_diagonal, accum, *refs):
-    tiles, rest = refs[: 2 * LATE], refs[2 * LATE :]
-    out, sums, left_dense, right_dense, cells, table, sem, rounded, out_sems = rest
-    place_pairs(tiles, left_dense, right_dense, cells, table, sem)
+def next_kernel(before, left_2, right_2, accum, *scratches):
+    left_dense, right_dense, cells, table, sem = scratches
+    place_pairs((left_2, right_2), left_dense, right_dense, cells, table, sem)
+    for low in range(0, TILE, WIDTH):
+        accum[:, low : low + WIDTH] = before[:, low : low + WIDTH] + multiply_pairs(left_dense, right_dense, low)
+
+
+def last_kernel(on_diagonal, accum, *refs):
+    out, sums, left_dense, right_dense, cells, table, sem, rounded, out_sems = refs[-9:]
+    place_pairs(refs[:-9], left_dense, right_dense, cells, table, sem)
     inside = lax.broadcasted_iota(jnp.int32, (BLK, BLK), 0) == lax.broadcasted_iota(jnp.int32, (BLK, BLK), 1)
     squares = jnp.zeros((8, WIDTH), jnp.float32)
     diagonal = jnp.zeros((8, BLK), jnp.float32)
@@ -147,8 +160,6 @@
 
 
 WHOLE = pl.BlockSpec(memory_space=pltpu.VMEM)
-EARLY = 2
-LATE = STEPS - EARLY
 CELLS = [pltpu.VMEM((8, LANES), jnp.int32), pltpu.SMEM((8, LANES), jnp.int32), pltpu.SemaphoreType.DMA]
 
 
@@ -164,34 +175,38 @@
     return [pltpu.VMEM(left_shape(steps), jnp.bfloat16), pltpu.VMEM(right_shape(steps), jnp.bfloat16)] + CELLS
 
 
-def multiply_early(tiles):
+LIMIT = pltpu.CompilerParams(vmem_limit_bytes=20 * 2**20)
+SMALL = pl.CostEstimate(flops=1000, bytes_accessed=1000, transcendentals=0)
+
+
+def multiply(kernel, name, inputs, steps):
     return pl.pallas_call(
-        early_kernel,
+        kernel,
         out_shape=jax.ShapeDtypeStruct((TILE, TILE), jnp.float32),
-        in_specs=[WHOLE] * len(tiles),
+        in_specs=[WHOLE] * len(inputs),
         out_specs=WHOLE,
-        scratch_shapes=scratch(EARLY),
-        compiler_params=pltpu.CompilerParams(vmem_limit_bytes=24 * 2**20),
-        cost_estimate=pl.CostEstimate(flops=2 * EARLY * TILE**3, bytes_accessed=5_000_000, transcendentals=0),
-        name="early_products",
-    )(*tiles)
-
-
-def multiply_late(on_diagonal, accum, tiles, fan):
+        scratch_shapes=scratch(steps),
+        compiler_params=LIMIT,
+        cost_estimate=SMALL,
+        name=name,
+    )(*inputs)
+
+
+def multiply_last(on_diagonal, inputs, fan):
     return pl.pallas_call(
-        late_kernel,
+        last_kernel,
         out_shape=(
             jax.ShapeDtypeStruct((TILE, TILE), jnp.bfloat16),
             jax.ShapeDtypeStruct((fan, LANES), jnp.float32),
         ),
-        in_specs=[pl.BlockSpec(memory_space=pltpu.SMEM)] + [WHOLE] * (1 + len(tiles)),
+        in_specs=[pl.BlockSpec(memory_space=pltpu.SMEM)] + [WHOLE] * len(inputs),
         out_specs=(pl.BlockSpec(memory_space=pl.ANY), WHOLE),
-        scratch_shapes=scratch(LATE)
+        scratch_shapes=scratch((len(inputs) - 1) // 2)
         + [pltpu.VMEM((TILE, TILE), jnp.bfloat16), pltpu.SemaphoreType.DMA((TILE // WIDTH,))],
-        compiler_params=pltpu.CompilerParams(vmem_limit_bytes=24 * 2**20),
-        cost_estimate=pl.CostEstimate(flops=2 * LATE * TILE**3, bytes_accessed=6_000_000, transcendentals=0),
-        name="late_products",
-    )(on_diagonal, accum, *tiles)
+        compiler_params=LIMIT,
+        cost_estimate=SMALL,
+        name="last_product",
+    )(on_diagonal, *inputs)
 
 
 def exchange(value, target, rows, cols):
@@ -220,9 +235,9 @@
     right_first = move(right, lambda i, j: (i - 1 if i % 2 else i - 3, j))
     left_middle = move(left_first, lambda i, j: (i, j - 1 if i % 2 == 0 else j + 1))
     right_second = move(right_middle, lambda i, j: (i ^ 1, j))
-    accum = multiply_early((left, right, left_first, right_first))
-    late = (left_middle, right_middle, left_second, right_second)
-    product, partial = multiply_late(on_diagonal, accum, late, rows)
+    accum = multiply(first_kernel, "first_products", (left, right, left_first, right_first), 2)
+    accum = multiply(next_kernel, "next_product", (accum, left_middle, right_middle), 1)
+    product, partial = multiply_last(on_diagonal, (accum, left_second, right_second), rows)
     row_sums = jnp.sum(spread_sum(partial, "row"), axis=0, keepdims=True)
     totals = jnp.sum(spread_sum(jnp.broadcast_to(row_sums, (cols, LANES)), "col"), axis=0)
     trace_scaled = totals[0] / math.sqrt(min(rows, cols) * TILE)

time: 125 us -> 124 us (level)
  starting transfers between devices: 41.2 us -> 51.2 us
  waiting for transfers between devices: 23.9 us -> 15.2 us
  blocking collectives: 39.9 us -> 38.1 us
    ppermute x6, starting transfers between devices: 41.2 us -> 51.2 us  [exchange(): return lax.ppermute(value, BOTH, pairs)]
    ppermute x6, waiting for transfers between devices: 23.9 us -> 15.2 us  [exchange(): return lax.ppermute(value, BOTH, pairs)]
    all_to_all x2, blocking collectives: 39.9 us -> 38.1 us  [spread_sum(): return lax.all_to_all(values, axis, 0, 0, tiled=True)]
    pallas_call x2 -> x3, Pallas kernels: 9.02 us -> 9.77 us  [the longest x2 5.64 us: multiply(): pl.pallas_call(kernel, out_shape=jax.ShapeDtypeStruct((TILE, TILE), jnp.f...]
  transfers between devices with their start and end apart: 6 -> 6, of which waited for: 1 -> 1; matrix products, arithmetic and copies ran while one was open for 0% -> 0% of each run, Pallas kernels for 3% -> 5%
where the time goes in v5:
time: 124 us
  starting transfers between devices  51.2 us (41%)
  blocking collectives  38.1 us (31%)
  waiting for transfers between devices  15.2 us (12%)
  Pallas kernels  11.9 us (10%)
  between operations  4.31 us (3%)
  local copies, waits for them, and re-layouts  2.73 us (2%)
    ppermute x6, starting transfers between devices, exchange(): return lax.ppermute(value, BOTH, pairs)  51.2 us
    all_to_all x2, blocking collectives, spread_sum(): return lax.all_to_all(values, axis, 0, 0, tiled=True)  38.1 us
    ppermute x6, waiting for transfers between devices, exchange(): return lax.ppermute(value, BOTH, pairs)  15.2 us
    pallas_call x2, Pallas kernels, multiply(): pl.pallas_call(kernel, out_shape=jax.ShapeDtypeStruct((TILE, TILE), jnp.f...  5.64 us
    pallas_call x1, Pallas kernels, multiply_last(): pl.pallas_call(last_kernel, out_shape=(jax.ShapeDtypeStruct((TILE, TILE),...  4.12 us
  transfers between devices with their start and end apart: 6, of which 1 were waited for; matrix products, arithmetic and copies ran while one was open for 0% of the time, Pallas kernels for 5%

profile of v5, /device:TPU:1, one launch (start us, length us, event | category | flops | bytes accessed | tf_op | source)
XLA Modules:
  0.0 123.5 jit_solution(6771122587229088763)
XLA Ops:
  0.6 2.2 %pack_tiles.1 = (bf16[2320,128]{1,0:T(8,128)(2,1)}, bf16[2320,128]{1,0:T(8,128)(2,1)}) custom-call(s32[1,18]{1,0:T(1,128)} %left_slots.1, s32[1,18]{1,0:T(1,128)} %right_slots.1, bf16[2304,128]{1,0:T(8,128)(2,1)} %bitcast.10, bf16[2304,128]{1,0:T(8,128)(2,1)} %bitcast.11), custom_call_target="tpu_custom_call" | custom-call | tf_op jit(solution)/shard_map/pack_tiles/pallas_call | solution.py:62
  2.8 7.6 %collective-permute-start = (bf16[2320,128]{1,0:T(8,128)(2,1)}, bf16[2320,128]{1,0:T(8,128)(2,1)S(1)}, u32[]{:S(2)}, u32[]{:S(2)}) collective-permute-start(bf16[2320,128]{1,0:T(8,128)(2,1)} %get-tuple-element.7.left_0), channel_id=1, source_target_pairs={{0,31},{1,0},{2,1},{3,2},{4,3},{5,4},{6,5},{7,6},{8,7},{9,8},{10,9... | collective-permute-start | bytes 1781768 | tf_op jit(solution)/shard_map/ppermute | solution.py:218
  10.4 19.4 %collective-permute-start.3 = (bf16[2320,128]{1,0:T(8,128)(2,1)}, bf16[2320,128]{1,0:T(8,128)(2,1)S(1)}, u32[]{:S(2)}, u32[]{:S(2)}) collective-permute-start(bf16[2320,128]{1,0:T(8,128)(2,1)} %get-tuple-element.8.right_0), channel_id=1, source_target_pairs={{0,960},{1,961},{2,962},{3,963},{4,964},{5,965},{6,966},{7,967},{8... | collective-permute-start | bytes 1781768 | tf_op jit(solution)/shard_map/ppermute | solution.py:218
  29.8 1.3 %collective-permute-start.1 = (bf16[2320,128]{1,0:T(8,128)(2,1)}, bf16[2320,128]{1,0:T(8,128)(2,1)S(1)}, u32[]{:S(2)}, u32[]{:S(2)}) collective-permute-start(bf16[2320,128]{1,0:T(8,128)(2,1)} %get-tuple-element.8.right_0), channel_id=1, source_target_pairs={{0,928},{1,929},{2,930},{3,931},{4,932},{5,933},{6,934},{7,935},{8... | collective-permute-start | bytes 1781768 | tf_op jit(solution)/shard_map/ppermute | solution.py:218
  31.1 0.0 collective-permute-done.left_1
  31.1 2.3 %collective-permute-start.2 = (bf16[2320,128]{1,0:T(8,128)(2,1)S(1)}, bf16[2320,128]{1,0:T(8,128)(2,1)S(1)}, u32[]{:S(2)}, u32[]{:S(2)}) collective-permute-start(bf16[2320,128]{1,0:T(8,128)(2,1)S(1)} %collective-permute-done.left_1), channel_id=1, source_target_pairs={{0,31},{1,0},{2,1},{3,2},{4,3},{5,4},{6,5},{7,6},{8,7},{9,8},{10,9... | collective-permute-start | bytes 1781768 | tf_op jit(solution)/shard_map/ppermute | solution.py:218
  33.4 7.2 %collective-permute-start.4 = (bf16[2320,128]{1,0:T(8,128)(2,1)}, bf16[2320,128]{1,0:T(8,128)(2,1)S(1)}, u32[]{:S(2)}, u32[]{:S(2)}) collective-permute-start(bf16[2320,128]{1,0:T(8,128)(2,1)} %get-tuple-element.7.left_0), channel_id=1, source_target_pairs={{0,29},{1,30},{2,31},{3,0},{4,1},{5,2},{6,3},{7,4},{8,5},{9,6},{10... | collective-permute-start | bytes 1781768 | tf_op jit(solution)/shard_map/ppermute | solution.py:218
  40.6 15.2 %collective-permute-done.3.right_2 = bf16[2320,128]{1,0:T(8,128)(2,1)S(1)} collective-permute-done((bf16[2320,128]{1,0:T(8,128)(2,1)}, bf16[2320,128]{1,0:T(8,128)(2,1)S(1)}, u32[]{:S(2)}, u32[]{:S(2)}) %collective-permute-start.3) | collective-permute-done | bytes 593952 | tf_op jit(solution)/shard_map/ppermute | solution.py:218
  55.8 13.4 %collective-permute-start.5 = (bf16[2320,128]{1,0:T(8,128)(2,1)S(1)}, bf16[2320,128]{1,0:T(8,128)(2,1)}, u32[]{:S(2)}, u32[]{:S(2)}) collective-permute-start(bf16[2320,128]{1,0:T(8,128)(2,1)S(1)} %collective-permute-done.3.right_2), channel_id=1, source_target_pairs={{0,32},{1,33},{2,34},{3,35},{4,36},{5,37},{6,38},{7,39},{8,40},{9,... | collective-permute-start | bytes 1781768 | tf_op jit(solution)/shard_map/ppermute | solution.py:218
  69.3 0.0 collective-permute-done.1.right_1
  69.3 0.0 copy-start
  69.3 1.1 copy-done
  70.3 0.0 copy-start.1
  70.3 1.1 copy-done.1
  71.4 3.5 %first_products.1.before = f32[768,768]{1,0:T(8,128)S(1)} custom-call(bf16[2320,128]{1,0:T(8,128)(2,1)S(1)} %copy-done, bf16[2320,128]{1,0:T(8,128)(2,1)S(1)} %copy-done.1, bf16[2320,128]{1,0:T(8,128)(2,1)S(1)} %collective-permute-done.left_1, bf16[2320,128]{1,0:T(8,128)(2,1)S(1)} %collective-permute-done.1.right_1), custom_call_target="tpu_custom_call" | custom-call | flops 1000 | bytes 1000 | tf_op jit(solution)/shard_map/first_products/pallas_call | solution.py:183
  74.9 0.0 collective-permute-done.2.left_2
  74.9 2.1 %next_product.1.accum = f32[768,768]{1,0:T(8,128)S(1)} custom-call(f32[768,768]{1,0:T(8,128)S(1)} %first_products.1.before, bf16[2320,128]{1,0:T(8,128)(2,1)S(1)} %collective-permute-done.2.left_2, bf16[2320,128]{1,0:T(8,128)(2,1)S(1)} %collective-permute-done.3.right_2), custom_call_target="tpu_custom_call" | custom-call | flops 1000 | bytes 1000 | tf_op jit(solution)/shard_map/next_product/pallas_call | solution.py:183
  77.1 0.0 collective-permute-done.4.refs_0_
  77.1 0.0 collective-permute-done.5.refs_1_
  77.1 4.1 %last_product.1 = (bf16[768,768]{1,0:T(8,128)(2,1)}, f32[32,128]{1,0:T(8,128)S(1)}) custom-call(s32[1]{0:T(128)} %bitcast.on_diagonal, f32[768,768]{1,0:T(8,128)S(1)} %next_product.1.accum, bf16[2320,128]{1,0:T(8,128)(2,1)S(1)} %collective-permute-done.4.refs_0_, bf16[2320,128]{1,0:T(8,128)(2,1)} %collective-permute-done.5.refs_1_), custom_call_target="tpu_custom_call" | custom-call | flops 1000 | bytes 1000 | tf_op jit(solution)/shard_map/last_product/pallas_call | solution.py:196
  81.2 21.3 %all_to_all.15 = f32[32,1,128]{2,1,0:T(1,128)S(1)} all-to-all(f32[32,1,128]{2,1,0:T(1,128)S(1)} %bitcast.9), channel_id=1, replica_groups=mesh['row'=32,'col'=32] {'row'}, dimensions={0} | all-to-all | bytes 32768 | tf_op jit(solution)/shard_map/all_to_all | solution.py:222
  102.6 0.1 reduce_sum.18
  102.6 16.7 %all_to_all.16 = f32[32,1,128]{2,1,0:T(1,128)S(1)} all-to-all(f32[32,1,128]{2,1,0:T(1,128)S(1)} %broadcast_in_dim.2), channel_id=1, replica_groups=mesh['row'=32,'col'=32] {'col'}, dimensions={0} | all-to-all | bytes 32768 | tf_op jit(solution)/shard_map/all_to_all | solution.py:222
  119.4 0.6 fusion
  (2 shorter events, 0.0 us)
Async XLA Ops:
  2.8 28.3 %collective-permute-start = (bf16[2320,128]{1,0:T(8,128)(2,1)}, bf16[2320,128]{1,0:T(8,128)(2,1)S(1)}, u32[]{:S(2)}, u32[]{:S(2)}) collective-permute-start(bf16[2320,128]{1,0:T(8,128)(2,1)} %get-tuple-element.7.left_0), channel_id=1, source_target_pairs={{0,31},{1,0},{2,1},{3,2},{4,3},{5,4},{6,5},{7,6},{8,7},{9,8},{10,9... | collective-permute-start | bytes 1781768 | tf_op jit(solution)/shard_map/ppermute | solution.py:218
  10.4 45.4 %collective-permute-start.3 = (bf16[2320,128]{1,0:T(8,128)(2,1)}, bf16[2320,128]{1,0:T(8,128)(2,1)S(1)}, u32[]{:S(2)}, u32[]{:S(2)}) collective-permute-start(bf16[2320,128]{1,0:T(8,128)(2,1)} %get-tuple-element.8.right_0), channel_id=1, source_target_pairs={{0,960},{1,961},{2,962},{3,963},{4,964},{5,965},{6,966},{7,967},{8... | collective-permute-start | bytes 1781768 | tf_op jit(solution)/shard_map/ppermute | solution.py:218
  29.8 39.5 %collective-permute-start.1 = (bf16[2320,128]{1,0:T(8,128)(2,1)}, bf16[2320,128]{1,0:T(8,128)(2,1)S(1)}, u32[]{:S(2)}, u32[]{:S(2)}) collective-permute-start(bf16[2320,128]{1,0:T(8,128)(2,1)} %get-tuple-element.8.right_0), channel_id=1, source_target_pairs={{0,928},{1,929},{2,930},{3,931},{4,932},{5,933},{6,934},{7,935},{8... | collective-permute-start | bytes 1781768 | tf_op jit(solution)/shard_map/ppermute | solution.py:218
  31.1 43.8 %collective-permute-start.2 = (bf16[2320,128]{1,0:T(8,128)(2,1)S(1)}, bf16[2320,128]{1,0:T(8,128)(2,1)S(1)}, u32[]{:S(2)}, u32[]{:S(2)}) collective-permute-start(bf16[2320,128]{1,0:T(8,128)(2,1)S(1)} %collective-permute-done.left_1), channel_id=1, source_target_pairs={{0,31},{1,0},{2,1},{3,2},{4,3},{5,4},{6,5},{7,6},{8,7},{9,8},{10,9... | collective-permute-start | bytes 1781768 | tf_op jit(solution)/shard_map/ppermute | solution.py:218
  33.4 43.7 %collective-permute-start.4 = (bf16[2320,128]{1,0:T(8,128)(2,1)}, bf16[2320,128]{1,0:T(8,128)(2,1)S(1)}, u32[]{:S(2)}, u32[]{:S(2)}) collective-permute-start(bf16[2320,128]{1,0:T(8,128)(2,1)} %get-tuple-element.7.left_0), channel_id=1, source_target_pairs={{0,29},{1,30},{2,31},{3,0},{4,1},{5,2},{6,3},{7,4},{8,5},{9,6},{10... | collective-permute-start | bytes 1781768 | tf_op jit(solution)/shard_map/ppermute | solution.py:218
  55.8 21.3 %collective-permute-start.5 = (bf16[2320,128]{1,0:T(8,128)(2,1)S(1)}, bf16[2320,128]{1,0:T(8,128)(2,1)}, u32[]{:S(2)}, u32[]{:S(2)}) collective-permute-start(bf16[2320,128]{1,0:T(8,128)(2,1)S(1)} %collective-permute-done.3.right_2), channel_id=1, source_target_pairs={{0,32},{1,33},{2,34},{3,35},{4,36},{5,37},{6,38},{7,39},{8,40},{9,... | collective-permute-start | bytes 1781768 | tf_op jit(solution)/shard_map/ppermute | solution.py:218
  69.3 1.1 copy-start
  70.3 1.1 copy-start.1

commit v6 on v5

--- a/solution.py
+++ b/solution.py
@@ -229,15 +229,16 @@
         left_slots, right_slots, left_blocks.reshape(-1, LANES), right_blocks.reshape(-1, LANES)
     )
     move = functools.partial(exchange, rows=rows, cols=cols)
+    right_middle = move(right, lambda i, j: (i - 2, j))
+    right_first = move(right, lambda i, j: (i - 1 if i % 2 else i - 3, j))
+    left, right_first = lax.optimization_barrier((left, right_first))
     left_first = move(left, lambda i, j: (i, j - 1 if i % 2 == 0 else j - 3))
-    right_middle = move(right, lambda i, j: (i - 2, j))
     left_second = move(left, lambda i, j: (i, j - 3 if i % 2 == 0 else j - 1))
-    right_first = move(right, lambda i, j: (i - 1 if i % 2 else i - 3, j))
     left_middle = move(left_first, lambda i, j: (i, j - 1 if i % 2 == 0 else j + 1))
     right_second = move(right_middle, lambda i, j: (i ^ 1, j))
     accum = multiply(first_kernel, "first_products", (left, right, left_first, right_first), 2)
-    accum = multiply(next_kernel, "next_product", (accum, left_middle, right_middle), 1)
-    product, partial = multiply_last(on_diagonal, (accum, left_second, right_second), rows)
+    accum = multiply(next_kernel, "next_product", (accum, left_second, right_second), 1)
+    product, partial = multiply_last(on_diagonal, (accum, left_middle, right_middle), rows)
     row_sums = jnp.sum(spread_sum(partial, "row"), axis=0, keepdims=True)
     totals = jnp.sum(spread_sum(jnp.broadcast_to(row_sums, (cols, LANES)), "col"), axis=0)
     trace_scaled = totals[0] / math.sqrt(min(rows, cols) * TILE)

time: 124 us -> 127 us (1.024)
  waiting for transfers between devices: 15.2 us -> 46.2 us
  starting transfers between devices: 51.2 us -> 34.2 us
  blocking collectives: 38.1 us -> 26.7 us
    ppermute x6, waiting for transfers between devices: 15.2 us -> 46.2 us  [exchange(): return lax.ppermute(value, BOTH, pairs)]
    ppermute x6, starting transfers between devices: 51.2 us -> 34.2 us  [exchange(): return lax.ppermute(value, BOTH, pairs)]
    all_to_all x2, blocking collectives: 38.1 us -> 26.7 us  [spread_sum(): return lax.all_to_all(values, axis, 0, 0, tiled=True)]
  transfers between devices with their start and end apart: 6 -> 6, of which waited for: 1 -> 3; matrix products, arithmetic and copies ran while one was open for 0% -> 0% of each run, Pallas kernels for 5% -> 4%
where the time goes in v6:
time: 127 us; the launch traced here: 126 us
  waiting for transfers between devices  46.2 us (36%)
  starting transfers between devices  34.2 us (27%)
  blocking collectives  26.7 us (21%)
  Pallas kernels  11.9 us (9%)
  between operations  4.3 us (3%)
  local copies, waits for them, and re-layouts  2.73 us (2%)
    ppermute x6, waiting for transfers between devices, exchange(): return lax.ppermute(value, BOTH, pairs)  46.2 us
    ppermute x6, starting transfers between devices, exchange(): return lax.ppermute(value, BOTH, pairs)  34.2 us
    all_to_all x2, blocking collectives, spread_sum(): return lax.all_to_all(values, axis, 0, 0, tiled=True)  26.7 us
    pallas_call x2, Pallas kernels, multiply(): pl.pallas_call(kernel, out_shape=jax.ShapeDtypeStruct((TILE, TILE), jnp.f...  5.64 us
    pallas_call x1, Pallas kernels, multiply_last(): pl.pallas_call(last_kernel, out_shape=(jax.ShapeDtypeStruct((TILE, TILE),...  4.12 us
  transfers between devices with their start and end apart: 6, of which 3 were waited for; matrix products, arithmetic and copies ran while one was open for 0% of the time, Pallas kernels for 4%

profile of v6, /device:TPU:1, one launch (start us, length us, event | category | flops | bytes accessed | tf_op | source)
XLA Modules:
  0.0 126.0 jit_solution(459187989710369553)
XLA Ops:
  0.6 2.2 %pack_tiles.1 = (bf16[2320,128]{1,0:T(8,128)(2,1)}, bf16[2320,128]{1,0:T(8,128)(2,1)}) custom-call(s32[1,18]{1,0:T(1,128)} %left_slots.1, s32[1,18]{1,0:T(1,128)} %right_slots.1, bf16[2304,128]{1,0:T(8,128)(2,1)} %bitcast.10, bf16[2304,128]{1,0:T(8,128)(2,1)} %bitcast.11), custom_call_target="tpu_custom_call" | custom-call | tf_op jit(solution)/shard_map/pack_tiles/pallas_call | solution.py:62
  2.8 14.2 %collective-permute-start = (bf16[2320,128]{1,0:T(8,128)(2,1)}, bf16[2320,128]{1,0:T(8,128)(2,1)S(1)}, u32[]{:S(2)}, u32[]{:S(2)}) collective-permute-start(bf16[2320,128]{1,0:T(8,128)(2,1)} %get-tuple-element.10.right_0), channel_id=1, source_target_pairs={{0,928},{1,929},{2,930},{3,931},{4,932},{5,933},{6,934},{7,935},{8... | collective-permute-start | bytes 1781768 | tf_op jit(solution)/shard_map/ppermute | solution.py:218
  17.0 5.5 %collective-permute-start.3 = (bf16[2320,128]{1,0:T(8,128)(2,1)}, bf16[2320,128]{1,0:T(8,128)(2,1)S(1)}, u32[]{:S(2)}, u32[]{:S(2)}) collective-permute-start(bf16[2320,128]{1,0:T(8,128)(2,1)} %get-tuple-element.10.right_0), channel_id=1, source_target_pairs={{0,960},{1,961},{2,962},{3,963},{4,964},{5,965},{6,966},{7,967},{8... | collective-permute-start | bytes 1781768 | tf_op jit(solution)/shard_map/ppermute | solution.py:218
  22.5 0.0 collective-permute-done.right_1
  22.5 6.8 %collective-permute-start.1 = (bf16[2320,128]{1,0:T(8,128)(2,1)}, bf16[2320,128]{1,0:T(8,128)(2,1)S(1)}, u32[]{:S(2)}, u32[]{:S(2)}) collective-permute-start(bf16[2320,128]{1,0:T(8,128)(2,1)} %get-tuple-element.11.left_0), channel_id=1, source_target_pairs={{0,31},{1,0},{2,1},{3,2},{4,3},{5,4},{6,5},{7,6},{8,7},{9,8},{10,9... | collective-permute-start | bytes 1781768 | tf_op jit(solution)/shard_map/ppermute | solution.py:218
  29.3 3.1 %collective-permute-start.2 = (bf16[2320,128]{1,0:T(8,128)(2,1)}, bf16[2320,128]{1,0:T(8,128)(2,1)S(1)}, u32[]{:S(2)}, u32[]{:S(2)}) collective-permute-start(bf16[2320,128]{1,0:T(8,128)(2,1)} %get-tuple-element.11.left_0), channel_id=1, source_target_pairs={{0,29},{1,30},{2,31},{3,0},{4,1},{5,2},{6,3},{7,4},{8,5},{9,6},{10... | collective-permute-start | bytes 1781768 | tf_op jit(solution)/shard_map/ppermute | solution.py:218
  32.4 16.0 %collective-permute-done.3.refs_1_ = bf16[2320,128]{1,0:T(8,128)(2,1)S(1)} collective-permute-done((bf16[2320,128]{1,0:T(8,128)(2,1)}, bf16[2320,128]{1,0:T(8,128)(2,1)S(1)}, u32[]{:S(2)}, u32[]{:S(2)}) %collective-permute-start.3) | collective-permute-done | bytes 593952 | tf_op jit(solution)/shard_map/ppermute | solution.py:218
  48.4 2.7 %collective-permute-start.4 = (bf16[2320,128]{1,0:T(8,128)(2,1)S(1)}, bf16[2320,128]{1,0:T(8,128)(2,1)S(1)}, u32[]{:S(2)}, u32[]{:S(2)}) collective-permute-start(bf16[2320,128]{1,0:T(8,128)(2,1)S(1)} %collective-permute-done.3.refs_1_), channel_id=1, source_target_pairs={{0,32},{1,33},{2,34},{3,35},{4,36},{5,37},{6,38},{7,39},{8,40},{9,... | collective-permute-start | bytes 1781768 | tf_op jit(solution)/shard_map/ppermute | solution.py:218
  51.1 25.0 %collective-permute-done.1.left_1 = bf16[2320,128]{1,0:T(8,128)(2,1)S(1)} collective-permute-done((bf16[2320,128]{1,0:T(8,128)(2,1)}, bf16[2320,128]{1,0:T(8,128)(2,1)S(1)}, u32[]{:S(2)}, u32[]{:S(2)}) %collective-permute-start.1) | collective-permute-done | bytes 593952 | tf_op jit(solution)/shard_map/ppermute | solution.py:218
  76.0 1.9 %collective-permute-start.5 = (bf16[2320,128]{1,0:T(8,128)(2,1)S(1)}, bf16[2320,128]{1,0:T(8,128)(2,1)}, u32[]{:S(2)}, u32[]{:S(2)}) collective-permute-start(bf16[2320,128]{1,0:T(8,128)(2,1)S(1)} %collective-permute-done.1.left_1), channel_id=1, source_target_pairs={{0,31},{1,0},{2,1},{3,2},{4,3},{5,4},{6,5},{7,6},{8,7},{9,8},{10,9... | collective-permute-start | bytes 1781768 | tf_op jit(solution)/shard_map/ppermute | solution.py:218
  78.0 0.0 copy-start
  78.0 1.1 copy-done
  79.0 0.0 copy-start.1
  79.0 1.1 copy-done.1
  80.1 3.5 %first_products.1.before = f32[768,768]{1,0:T(8,128)S(1)} custom-call(bf16[2320,128]{1,0:T(8,128)(2,1)S(1)} %copy-done, bf16[2320,128]{1,0:T(8,128)(2,1)S(1)} %copy-done.1, bf16[2320,128]{1,0:T(8,128)(2,1)S(1)} %collective-permute-done.1.left_1, bf16[2320,128]{1,0:T(8,128)(2,1)S(1)} %collective-permute-done.right_1), custom_call_target="tpu_custom_call" | custom-call | flops 1000 | bytes 1000 | tf_op jit(solution)/shard_map/first_products/pallas_call | solution.py:183
  83.6 0.0 collective-permute-done.2.left_2
  83.6 0.0 collective-permute-done.4.right_2
  83.6 2.1 %next_product.1.accum = f32[768,768]{1,0:T(8,128)S(1)} custom-call(f32[768,768]{1,0:T(8,128)S(1)} %first_products.1.before, bf16[2320,128]{1,0:T(8,128)(2,1)S(1)} %collective-permute-done.2.left_2, bf16[2320,128]{1,0:T(8,128)(2,1)S(1)} %collective-permute-done.4.right_2), custom_call_target="tpu_custom_call" | custom-call | flops 1000 | bytes 1000 | tf_op jit(solution)/shard_map/next_product/pallas_call | solution.py:183
  85.8 5.2 %collective-permute-done.5.refs_0_ = bf16[2320,128]{1,0:T(8,128)(2,1)} collective-permute-done((bf16[2320,128]{1,0:T(8,128)(2,1)S(1)}, bf16[2320,128]{1,0:T(8,128)(2,1)}, u32[]{:S(2)}, u32[]{:S(2)}) %collective-permute-start.5) | collective-permute-done | bytes 593952 | tf_op jit(solution)/shard_map/ppermute | solution.py:218
  91.0 4.1 %last_product.1 = (bf16[768,768]{1,0:T(8,128)(2,1)}, f32[32,128]{1,0:T(8,128)S(1)}) custom-call(s32[1]{0:T(128)} %bitcast.on_diagonal, f32[768,768]{1,0:T(8,128)S(1)} %next_product.1.accum, bf16[2320,128]{1,0:T(8,128)(2,1)} %collective-permute-done.5.refs_0_, bf16[2320,128]{1,0:T(8,128)(2,1)S(1)} %collective-permute-done.3.refs_1_), custom_call_target="tpu_custom_call" | custom-call | flops 1000 | bytes 1000 | tf_op jit(solution)/shard_map/last_product/pallas_call | solution.py:196
  95.2 9.6 %all_to_all.15 = f32[32,1,128]{2,1,0:T(1,128)S(1)} all-to-all(f32[32,1,128]{2,1,0:T(1,128)S(1)} %bitcast.9), channel_id=1, replica_groups=mesh['row'=32,'col'=32] {'row'}, dimensions={0} | all-to-all | bytes 32768 | tf_op jit(solution)/shard_map/all_to_all | solution.py:222
  104.7 0.1 reduce_sum.18
  104.8 17.1 %all_to_all.16 = f32[32,1,128]{2,1,0:T(1,128)S(1)} all-to-all(f32[32,1,128]{2,1,0:T(1,128)S(1)} %broadcast_in_dim.2), channel_id=1, replica_groups=mesh['row'=32,'col'=32] {'col'}, dimensions={0} | all-to-all | bytes 32768 | tf_op jit(solution)/shard_map/all_to_all | solution.py:222
  121.9 0.6 fusion
  (2 shorter events, 0.0 us)
Async XLA Ops:
  2.8 19.7 %collective-permute-start = (bf16[2320,128]{1,0:T(8,128)(2,1)}, bf16[2320,128]{1,0:T(8,128)(2,1)S(1)}, u32[]{:S(2)}, u32[]{:S(2)}) collective-permute-start(bf16[2320,128]{1,0:T(8,128)(2,1)} %get-tuple-element.10.right_0), channel_id=1, source_target_pairs={{0,928},{1,929},{2,930},{3,931},{4,932},{5,933},{6,934},{7,935},{8... | collective-permute-start | bytes 1781768 | tf_op jit(solution)/shard_map/ppermute | solution.py:218
  17.0 31.4 %collective-permute-start.3 = (bf16[2320,128]{1,0:T(8,128)(2,1)}, bf16[2320,128]{1,0:T(8,128)(2,1)S(1)}, u32[]{:S(2)}, u32[]{:S(2)}) collective-permute-start(bf16[2320,128]{1,0:T(8,128)(2,1)} %get-tuple-element.10.right_0), channel_id=1, source_target_pairs={{0,960},{1,961},{2,962},{3,963},{4,964},{5,965},{6,966},{7,967},{8... | collective-permute-start | bytes 1781768 | tf_op jit(solution)/shard_map/ppermute | solution.py:218
  22.5 53.6 %collective-permute-start.1 = (bf16[2320,128]{1,0:T(8,128)(2,1)}, bf16[2320,128]{1,0:T(8,128)(2,1)S(1)}, u32[]{:S(2)}, u32[]{:S(2)}) collective-permute-start(bf16[2320,128]{1,0:T(8,128)(2,1)} %get-tuple-element.11.left_0), channel_id=1, source_target_pairs={{0,31},{1,0},{2,1},{3,2},{4,3},{5,4},{6,5},{7,6},{8,7},{9,8},{10,9... | collective-permute-start | bytes 1781768 | tf_op jit(solution)/shard_map/ppermute | solution.py:218
  29.3 54.4 %collective-permute-start.2 = (bf16[2320,128]{1,0:T(8,128)(2,1)}, bf16[2320,128]{1,0:T(8,128)(2,1)S(1)}, u32[]{:S(2)}, u32[]{:S(2)}) collective-permute-start(bf16[2320,128]{1,0:T(8,128)(2,1)} %get-tuple-element.11.left_0), channel_id=1, source_target_pairs={{0,29},{1,30},{2,31},{3,0},{4,1},{5,2},{6,3},{7,4},{8,5},{9,6},{10... | collective-permute-start | bytes 1781768 | tf_op jit(solution)/shard_map/ppermute | solution.py:218
  48.4 35.3 %collective-permute-start.4 = (bf16[2320,128]{1,0:T(8,128)(2,1)S(1)}, bf16[2320,128]{1,0:T(8,128)(2,1)S(1)}, u32[]{:S(2)}, u32[]{:S(2)}) collective-permute-start(bf16[2320,128]{1,0:T(8,128)(2,1)S(1)} %collective-permute-done.3.refs_1_), channel_id=1, source_target_pairs={{0,32},{1,33},{2,34},{3,35},{4,36},{5,37},{6,38},{7,39},{8,40},{9,... | collective-permute-start | bytes 1781768 | tf_op jit(solution)/shard_map/ppermute | solution.py:218
  76.0 15.0 %collective-permute-start.5 = (bf16[2320,128]{1,0:T(8,128)(2,1)S(1)}, bf16[2320,128]{1,0:T(8,128)(2,1)}, u32[]{:S(2)}, u32[]{:S(2)}) collective-permute-start(bf16[2320,128]{1,0:T(8,128)(2,1)S(1)} %collective-permute-done.1.left_1), channel_id=1, source_target_pairs={{0,31},{1,0},{2,1},{3,2},{4,3},{5,4},{6,5},{7,6},{8,7},{9,8},{10,9... | collective-permute-start | bytes 1781768 | tf_op jit(solution)/shard_map/ppermute | solution.py:218
  78.0 1.1 copy-start
  79.0 1.1 copy-start.1

commit v7 on v5

--- a/solution.py
+++ b/solution.py
@@ -115,29 +115,22 @@
         accum[:, low : low + WIDTH] = before[:, low : low + WIDTH] + multiply_pairs(left_dense, right_dense, low)
 
 
-def last_kernel(on_diagonal, accum, *refs):
-    out, sums, left_dense, right_dense, cells, table, sem, rounded, out_sems = refs[-9:]
-    place_pairs(refs[:-9], left_dense, right_dense, cells, table, sem)
-    inside = lax.broadcasted_iota(jnp.int32, (BLK, BLK), 0) == lax.broadcasted_iota(jnp.int32, (BLK, BLK), 1)
-    squares = jnp.zeros((8, WIDTH), jnp.float32)
-    diagonal = jnp.zeros((8, BLK), jnp.float32)
-    copies = []
-    for part in range(TILE // WIDTH):
-        low = part * WIDTH
-        columns = pl.ds(low, WIDTH)
+def last_kernel(on_diagonal, accum, left_3, right_3, out, sums, *scratches):
+    left_dense, right_dense, cells, table, sem = scratches
+    place_pairs((left_3, right_3), left_dense, right_dense, cells, table, sem)
+    square_sum = jnp.float32(0)
+    diagonal_sum = jnp.float32(0)
+    inside = lax.broadcasted_iota(jnp.int32, (WIDTH, WIDTH), 0) == lax.broadcasted_iota(
+        jnp.int32, (WIDTH, WIDTH), 1
+    )
+    for low in range(0, TILE, WIDTH):
         total = accum[:, low : low + WIDTH] + multiply_pairs(left_dense, right_dense, low)
-        rounded[:, low : low + WIDTH] = total.astype(rounded.dtype)
-        copies.append(pltpu.make_async_copy(rounded.at[:, columns], out.at[:, columns], out_sems.at[part]))
-        copies[-1].start()
-        squares += jnp.sum((total * total).reshape(-1, 8, WIDTH), axis=0)
-        for block in range(0, WIDTH, BLK):
-            corner = total[low + block : low + block + BLK, block : block + BLK]
-            diagonal += jnp.sum(jnp.where(inside, corner, 0.0).reshape(-1, 8, BLK), axis=0)
-    diagonal_sum = jnp.where(on_diagonal[0] > 0, jnp.sum(diagonal), 0.0)
+        out[:, low : low + WIDTH] = total.astype(out.dtype)
+        square_sum += jnp.sum(total * total)
+        diagonal_sum += jnp.sum(jnp.where(inside, total[low : low + WIDTH, :], 0.0))
+    diagonal_sum = jnp.where(on_diagonal[0] > 0, diagonal_sum, 0.0)
     lane = lax.broadcasted_iota(jnp.int32, sums.shape, 1)
-    sums[...] = jnp.where(lane == 0, diagonal_sum, jnp.where(lane == 1, jnp.sum(squares), 0.0))
-    for copy in copies:
-        copy.wait()
+    sums[...] = jnp.where(lane == 0, diagonal_sum, jnp.where(lane == 1, square_sum, 0.0))
 
 
 def place_pairs(tiles, left_dense, right_dense, cells, table, sem):
@@ -200,9 +193,8 @@
             jax.ShapeDtypeStruct((fan, LANES), jnp.float32),
         ),
         in_specs=[pl.BlockSpec(memory_space=pltpu.SMEM)] + [WHOLE] * len(inputs),
-        out_specs=(pl.BlockSpec(memory_space=pl.ANY), WHOLE),
-        scratch_shapes=scratch((len(inputs) - 1) // 2)
-        + [pltpu.VMEM((TILE, TILE), jnp.bfloat16), pltpu.SemaphoreType.DMA((TILE // WIDTH,))],
+        out_specs=(WHOLE, WHOLE),
+        scratch_shapes=scratch(1),
         compiler_params=LIMIT,
         cost_estimate=SMALL,
         name="last_product",
@@ -230,12 +222,13 @@
     )
     move = functools.partial(exchange, rows=rows, cols=cols)
     left_first = move(left, lambda i, j: (i, j - 1 if i % 2 == 0 else j - 3))
+    left_second = move(left, lambda i, j: (i, j - 3 if i % 2 == 0 else j - 1))
+    left_middle = move(left_first, lambda i, j: (i, j - 1 if i % 2 == 0 else j + 1))
+    right_first = move(right, lambda i, j: (i - 1 if i % 2 else i - 3, j))
     right_middle = move(right, lambda i, j: (i - 2, j))
-    left_second = move(left, lambda i, j: (i, j - 3 if i % 2 == 0 else j - 1))
-    right_first = move(right, lambda i, j: (i - 1 if i % 2 else i - 3, j))
-    left_middle = move(left_first, lambda i, j: (i, j - 1 if i % 2 == 0 else j + 1))
+    accum = multiply(first_kernel, "first_products", (left, right, left_first, right_first), 2)
+    right_middle, accum = lax.optimization_barrier((right_middle, accum))
     right_second = move(right_middle, lambda i, j: (i ^ 1, j))
-    accum = multiply(first_kernel, "first_products", (left, right, left_first, right_first), 2)
     accum = multiply(next_kernel, "next_product", (accum, left_middle, right_middle), 1)
     product, partial = multiply_last(on_diagonal, (accum, left_second, right_second), rows)
     row_sums = jnp.sum(spread_sum(partial, "row"), axis=0, keepdims=True)

time: 124 us -> 123 us (level)
  starting transfers between devices: 51.2 us -> 36.5 us
  waiting for transfers between devices: 15.2 us -> 27.2 us
  Pallas kernels: 11.9 us -> 13.3 us
    ppermute x6, starting transfers between devices: 51.2 us -> 36.5 us  [exchange(): return lax.ppermute(value, BOTH, pairs)]
    ppermute x6, waiting for transfers between devices: 15.2 us -> 27.2 us  [exchange(): return lax.ppermute(value, BOTH, pairs)]
where the time goes in v7:
time: 123 us
  blocking collectives  38.4 us (31%)
  starting transfers between devices  36.5 us (30%)
  waiting for transfers between devices  27.2 us (22%)
  Pallas kernels  13.3 us (11%)
  between operations  4.32 us (4%)
  local copies, waits for them, and re-layouts  2.73 us (2%)
    all_to_all x2, blocking collectives, spread_sum(): return lax.all_to_all(values, axis, 0, 0, tiled=True)  38.4 us
    ppermute x6, starting transfers between devices, exchange(): return lax.ppermute(value, BOTH, pairs)  36.5 us
    ppermute x6, waiting for transfers between devices, exchange(): return lax.ppermute(value, BOTH, pairs)  27.2 us
    pallas_call x2, Pallas kernels, multiply(): pl.pallas_call(kernel, out_shape=jax.ShapeDtypeStruct((TILE, TILE), jnp.f...  6.7 us
    pallas_call x1, Pallas kernels, multiply_last(): pl.pallas_call(last_kernel, out_shape=(jax.ShapeDtypeStruct((TILE, TILE),...  4.4 us
  transfers between devices with their start and end apart: 6, of which 1 were waited for; matrix products, arithmetic and copies ran while one was open for 0% of the time, Pallas kernels for 5%

profile of v7, /device:TPU:1, one launch (start us, length us, event | category | flops | bytes accessed | tf_op | source)
XLA Modules:
  0.0 122.5 jit_solution(1622315614418250061)
XLA Ops:
  0.6 2.2 %pack_tiles.1 = (bf16[2320,128]{1,0:T(8,128)(2,1)}, bf16[2320,128]{1,0:T(8,128)(2,1)}) custom-call(s32[1,18]{1,0:T(1,128)} %left_slots.1, s32[1,18]{1,0:T(1,128)} %right_slots.1, bf16[2304,128]{1,0:T(8,128)(2,1)} %bitcast.10, bf16[2304,128]{1,0:T(8,128)(2,1)} %bitcast.11), custom_call_target="tpu_custom_call" | custom-call | tf_op jit(solution)/shard_map/pack_tiles/pallas_call | solution.py:62
  2.8 7.6 %collective-permute-start.1 = (bf16[2320,128]{1,0:T(8,128)(2,1)}, bf16[2320,128]{1,0:T(8,128)(2,1)S(1)}, u32[]{:S(2)}, u32[]{:S(2)}) collective-permute-start(bf16[2320,128]{1,0:T(8,128)(2,1)} %get-tuple-element.10.left_0), channel_id=1, source_target_pairs={{0,31},{1,0},{2,1},{3,2},{4,3},{5,4},{6,5},{7,6},{8,7},{9,8},{10,9... | collective-permute-start | bytes 1781768 | tf_op jit(solution)/shard_map/ppermute | solution.py:210
  10.4 8.5 %collective-permute-start.2 = (bf16[2320,128]{1,0:T(8,128)(2,1)}, bf16[2320,128]{1,0:T(8,128)(2,1)S(1)}, u32[]{:S(2)}, u32[]{:S(2)}) collective-permute-start(bf16[2320,128]{1,0:T(8,128)(2,1)} %get-tuple-element.9.right_0), channel_id=1, source_target_pairs={{0,928},{1,929},{2,930},{3,931},{4,932},{5,933},{6,934},{7,935},{8... | collective-permute-start | bytes 1781768 | tf_op jit(solution)/shard_map/ppermute | solution.py:210
  18.9 11.9 %collective-permute-start = (bf16[2320,128]{1,0:T(8,128)(2,1)}, bf16[2320,128]{1,0:T(8,128)(2,1)S(1)}, u32[]{:S(2)}, u32[]{:S(2)}) collective-permute-start(bf16[2320,128]{1,0:T(8,128)(2,1)} %get-tuple-element.9.right_0), channel_id=1, source_target_pairs={{0,960},{1,961},{2,962},{3,963},{4,964},{5,965},{6,966},{7,967},{8... | collective-permute-start | bytes 1781768 | tf_op jit(solution)/shard_map/ppermute | solution.py:210
  30.8 3.6 %collective-permute-start.4 = (bf16[2320,128]{1,0:T(8,128)(2,1)}, bf16[2320,128]{1,0:T(8,128)(2,1)}, u32[]{:S(2)}, u32[]{:S(2)}) collective-permute-start(bf16[2320,128]{1,0:T(8,128)(2,1)} %get-tuple-element.10.left_0), channel_id=1, source_target_pairs={{0,29},{1,30},{2,31},{3,0},{4,1},{5,2},{6,3},{7,4},{8,5},{9,6},{10... | collective-permute-start | bytes 1781768 | tf_op jit(solution)/shard_map/ppermute | solution.py:210
  34.4 0.0 collective-permute-done.1.left_1
  34.4 2.6 %collective-permute-start.3 = (bf16[2320,128]{1,0:T(8,128)(2,1)S(1)}, bf16[2320,128]{1,0:T(8,128)(2,1)}, u32[]{:S(2)}, u32[]{:S(2)}) collective-permute-start(bf16[2320,128]{1,0:T(8,128)(2,1)S(1)} %collective-permute-done.1.left_1), channel_id=1, source_target_pairs={{0,31},{1,0},{2,1},{3,2},{4,3},{5,4},{6,5},{7,6},{8,7},{9,8},{10,9... | collective-permute-start | bytes 1781768 | tf_op jit(solution)/shard_map/ppermute | solution.py:210
  37.0 0.0 collective-permute-done.2.right_1
  37.0 0.0 copy-start
  37.0 1.1 copy-done
  38.1 0.0 copy-start.1
  38.1 1.1 copy-done.1
  39.2 3.5 %first_products.1.before = f32[768,768]{1,0:T(8,128)S(1)} custom-call(bf16[2320,128]{1,0:T(8,128)(2,1)S(1)} %copy-done, bf16[2320,128]{1,0:T(8,128)(2,1)S(1)} %copy-done.1, bf16[2320,128]{1,0:T(8,128)(2,1)S(1)} %collective-permute-done.1.left_1, bf16[2320,128]{1,0:T(8,128)(2,1)S(1)} %collective-permute-done.2.right_1), custom_call_target="tpu_custom_call" | custom-call | flops 1000 | bytes 1000 | tf_op jit(solution)/shard_map/first_products/pallas_call | solution.py:176
  42.7 27.2 %collective-permute-done.right_2 = bf16[2320,128]{1,0:T(8,128)(2,1)S(1)} collective-permute-done((bf16[2320,128]{1,0:T(8,128)(2,1)}, bf16[2320,128]{1,0:T(8,128)(2,1)S(1)}, u32[]{:S(2)}, u32[]{:S(2)}) %collective-permute-start) | collective-permute-done | bytes 593952 | tf_op jit(solution)/shard_map/ppermute | solution.py:210
  69.9 2.4 %collective-permute-start.5 = (bf16[2320,128]{1,0:T(8,128)(2,1)S(1)}, bf16[2320,128]{1,0:T(8,128)(2,1)}, u32[]{:S(2)}, u32[]{:S(2)}) collective-permute-start(bf16[2320,128]{1,0:T(8,128)(2,1)S(1)} %collective-permute-done.right_2), channel_id=1, source_target_pairs={{0,32},{1,33},{2,34},{3,35},{4,36},{5,37},{6,38},{7,39},{8,40},{9,... | collective-permute-start | bytes 1781768 | tf_op jit(solution)/shard_map/ppermute | solution.py:210
  72.3 0.0 collective-permute-done.3.left_2
  72.3 3.2 %next_product.1.accum = f32[768,768]{1,0:T(8,128)S(1)} custom-call(f32[768,768]{1,0:T(8,128)S(1)} %first_products.1.before, bf16[2320,128]{1,0:T(8,128)(2,1)} %collective-permute-done.3.left_2, bf16[2320,128]{1,0:T(8,128)(2,1)S(1)} %collective-permute-done.right_2), custom_call_target="tpu_custom_call" | custom-call | flops 1000 | bytes 1000 | tf_op jit(solution)/shard_map/next_product/pallas_call | solution.py:176
  75.5 0.0 collective-permute-done.4.left_3
  75.5 0.0 collective-permute-done.5.right_3
  75.5 4.4 %last_product.1 = (bf16[768,768]{1,0:T(8,128)(2,1)}, f32[32,128]{1,0:T(8,128)S(1)}) custom-call(s32[1]{0:T(128)} %bitcast.on_diagonal, f32[768,768]{1,0:T(8,128)S(1)} %next_product.1.accum, bf16[2320,128]{1,0:T(8,128)(2,1)} %collective-permute-done.4.left_3, bf16[2320,128]{1,0:T(8,128)(2,1)} %collective-permute-done.5.right_3), custom_call_target="tpu_custom_call" | custom-call | flops 1000 | bytes 1000 | tf_op jit(solution)/shard_map/last_product/pallas_call | solution.py:189
  79.9 19.6 %all_to_all.15 = f32[32,1,128]{2,1,0:T(1,128)S(1)} all-to-all(f32[32,1,128]{2,1,0:T(1,128)S(1)} %bitcast.9), channel_id=1, replica_groups=mesh['row'=32,'col'=32] {'row'}, dimensions={0} | all-to-all | bytes 32768 | tf_op jit(solution)/shard_map/all_to_all | solution.py:214
  99.6 0.1 reduce_sum.18
  99.6 18.7 %all_to_all.16 = f32[32,1,128]{2,1,0:T(1,128)S(1)} all-to-all(f32[32,1,128]{2,1,0:T(1,128)S(1)} %broadcast_in_dim.2), channel_id=1, replica_groups=mesh['row'=32,'col'=32] {'col'}, dimensions={0} | all-to-all | bytes 32768 | tf_op jit(solution)/shard_map/all_to_all | solution.py:214
  118.4 0.6 fusion
  (2 shorter events, 0.0 us)
Async XLA Ops:
  2.8 31.6 %collective-permute-start.1 = (bf16[2320,128]{1,0:T(8,128)(2,1)}, bf16[2320,128]{1,0:T(8,128)(2,1)S(1)}, u32[]{:S(2)}, u32[]{:S(2)}) collective-permute-start(bf16[2320,128]{1,0:T(8,128)(2,1)} %get-tuple-element.10.left_0), channel_id=1, source_target_pairs={{0,31},{1,0},{2,1},{3,2},{4,3},{5,4},{6,5},{7,6},{8,7},{9,8},{10,9... | collective-permute-start | bytes 1781768 | tf_op jit(solution)/shard_map/ppermute | solution.py:210
  10.4 26.6 %collective-permute-start.2 = (bf16[2320,128]{1,0:T(8,128)(2,1)}, bf16[2320,128]{1,0:T(8,128)(2,1)S(1)}, u32[]{:S(2)}, u32[]{:S(2)}) collective-permute-start(bf16[2320,128]{1,0:T(8,128)(2,1)} %get-tuple-element.9.right_0), channel_id=1, source_target_pairs={{0,928},{1,929},{2,930},{3,931},{4,932},{5,933},{6,934},{7,935},{8... | collective-permute-start | bytes 1781768 | tf_op jit(solution)/shard_map/ppermute | solution.py:210
  18.9 51.0 %collective-permute-start = (bf16[2320,128]{1,0:T(8,128)(2,1)}, bf16[2320,128]{1,0:T(8,128)(2,1)S(1)}, u32[]{:S(2)}, u32[]{:S(2)}) collective-permute-start(bf16[2320,128]{1,0:T(8,128)(2,1)} %get-tuple-element.9.right_0), channel_id=1, source_target_pairs={{0,960},{1,961},{2,962},{3,963},{4,964},{5,965},{6,966},{7,967},{8... | collective-permute-start | bytes 1781768 | tf_op jit(solution)/shard_map/ppermute | solution.py:210
  30.8 44.7 %collective-permute-start.4 = (bf16[2320,128]{1,0:T(8,128)(2,1)}, bf16[2320,128]{1,0:T(8,128)(2,1)}, u32[]{:S(2)}, u32[]{:S(2)}) collective-permute-start(bf16[2320,128]{1,0:T(8,128)(2,1)} %get-tuple-element.10.left_0), channel_id=1, source_target_pairs={{0,29},{1,30},{2,31},{3,0},{4,1},{5,2},{6,3},{7,4},{8,5},{9,6},{10... | collective-permute-start | bytes 1781768 | tf_op jit(solution)/shard_map/ppermute | solution.py:210
  34.4 37.9 %collective-permute-start.3 = (bf16[2320,128]{1,0:T(8,128)(2,1)S(1)}, bf16[2320,128]{1,0:T(8,128)(2,1)}, u32[]{:S(2)}, u32[]{:S(2)}) collective-permute-start(bf16[2320,128]{1,0:T(8,128)(2,1)S(1)} %collective-permute-done.1.left_1), channel_id=1, source_target_pairs={{0,31},{1,0},{2,1},{3,2},{4,3},{5,4},{6,5},{7,6},{8,7},{9,8},{10,9... | collective-permute-start | bytes 1781768 | tf_op jit(solution)/shard_map/ppermute | solution.py:210
  37.0 1.1 copy-start
  38.1 1.1 copy-start.1
  69.9 5.6 %collective-permute-start.5 = (bf16[2320,128]{1,0:T(8,128)(2,1)S(1)}, bf16[2320,128]{1,0:T(8,128)(2,1)}, u32[]{:S(2)}, u32[]{:S(2)}) collective-permute-start(bf16[2320,128]{1,0:T(8,128)(2,1)S(1)} %collective-permute-done.right_2), channel_id=1, source_target_pairs={{0,32},{1,33},{2,34},{3,35},{4,36},{5,37},{6,38},{7,39},{8,40},{9,... | collective-permute-start | bytes 1781768 | tf_op jit(solution)/shard_map/ppermute | solution.py:210

commit v8 on v7

--- a/solution.py
+++ b/solution.py
@@ -108,14 +108,11 @@
         accum[:, low : low + WIDTH] = multiply_pairs(left_dense, right_dense, low)
 
 
-def next_kernel(before, left_2, right_2, accum, *scratches):
-    left_dense, right_dense, cells, table, sem = scratches
+def place_kernel(left_2, right_2, left_dense, right_dense, cells, table, sem):
     place_pairs((left_2, right_2), left_dense, right_dense, cells, table, sem)
-    for low in range(0, TILE, WIDTH):
-        accum[:, low : low + WIDTH] = before[:, low : low + WIDTH] + multiply_pairs(left_dense, right_dense, low)
-
-
-def last_kernel(on_diagonal, accum, left_3, right_3, out, sums, *scratches):
+
+
+def last_kernel(on_diagonal, accum, left_early, right_early, left_3, right_3, out, sums, *scratches):
     left_dense, right_dense, cells, table, sem = scratches
     place_pairs((left_3, right_3), left_dense, right_dense, cells, table, sem)
     square_sum = jnp.float32(0)
@@ -124,7 +121,8 @@
         jnp.int32, (WIDTH, WIDTH), 1
     )
     for low in range(0, TILE, WIDTH):
-        total = accum[:, low : low + WIDTH] + multiply_pairs(left_dense, right_dense, low)
+        total = accum[:, low : low + WIDTH] + multiply_pairs(left_early, right_early, low)
+        total += multiply_pairs(left_dense, right_dense, low)
         out[:, low : low + WIDTH] = total.astype(out.dtype)
         square_sum += jnp.sum(total * total)
         diagonal_sum += jnp.sum(jnp.where(inside, total[low : low + WIDTH, :], 0.0))
@@ -168,7 +166,7 @@
     return [pltpu.VMEM(left_shape(steps), jnp.bfloat16), pltpu.VMEM(right_shape(steps), jnp.bfloat16)] + CELLS
 
 
-LIMIT = pltpu.CompilerParams(vmem_limit_bytes=20 * 2**20)
+LIMIT = pltpu.CompilerParams(vmem_limit_bytes=14 * 2**20)
 SMALL = pl.CostEstimate(flops=1000, bytes_accessed=1000, transcendentals=0)
 
 
@@ -182,6 +180,22 @@
         compiler_params=LIMIT,
         cost_estimate=SMALL,
         name=name,
+    )(*inputs)
+
+
+def place_only(inputs):
+    return pl.pallas_call(
+        place_kernel,
+        out_shape=(
+            jax.ShapeDtypeStruct(left_shape(1), jnp.bfloat16),
+            jax.ShapeDtypeStruct(right_shape(1), jnp.bfloat16),
+        ),
+        in_specs=[WHOLE] * 2,
+        out_specs=(WHOLE, WHOLE),
+        scratch_shapes=CELLS,
+        compiler_params=LIMIT,
+        cost_estimate=SMALL,
+        name="place_forwarded",
     )(*inputs)
 
 
@@ -229,8 +243,8 @@
     accum = multiply(first_kernel, "first_products", (left, right, left_first, right_first), 2)
     right_middle, accum = lax.optimization_barrier((right_middle, accum))
     right_second = move(right_middle, lambda i, j: (i ^ 1, j))
-    accum = multiply(next_kernel, "next_product", (accum, left_middle, right_middle), 1)
-    product, partial = multiply_last(on_diagonal, (accum, left_second, right_second), rows)
+    placed = place_only((left_middle, right_middle))
+    product, partial = multiply_last(on_diagonal, (accum, *placed, left_second, right_second), rows)
     row_sums = jnp.sum(spread_sum(partial, "row"), axis=0, keepdims=True)
     totals = jnp.sum(spread_sum(jnp.broadcast_to(row_sums, (cols, LANES)), "col"), axis=0)
     trace_scaled = totals[0] / math.sqrt(min(rows, cols) * TILE)

time: 123 us -> 122 us (level)
    pallas_call x2 -> x1, Pallas kernels: 6.7 us -> 4.56 us  [multiply(): pl.pallas_call(kernel, out_shape=jax.ShapeDtypeStruct((TILE, TILE), jnp.f...]
  transfers between devices with their start and end apart: 6 -> 6, of which waited for: 1 -> 2; matrix products, arithmetic and copies ran while one was open for 0% -> 0% of each run, Pallas kernels for 5% -> 5%
where the time goes in v8:
time: 122 us; the launch traced here: 121 us
  blocking collectives  37.7 us (31%)
  starting transfers between devices  36.6 us (30%)
  waiting for transfers between devices  26.8 us (22%)
  Pallas kernels  13.2 us (11%)
  between operations  4.31 us (4%)
  local copies, waits for them, and re-layouts  2.73 us (2%)
    all_to_all x2, blocking collectives, spread_sum(): return lax.all_to_all(values, axis, 0, 0, tiled=True)  37.7 us
    ppermute x6, starting transfers between devices, exchange(): return lax.ppermute(value, BOTH, pairs)  36.6 us
    ppermute x6, waiting for transfers between devices, exchange(): return lax.ppermute(value, BOTH, pairs)  26.8 us
    pallas_call x1, Pallas kernels, multiply_last(): pl.pallas_call(last_kernel, out_shape=(jax.ShapeDtypeStruct((TILE, TILE),...  5.34 us
    pallas_call x1, Pallas kernels, multiply(): pl.pallas_call(kernel, out_shape=jax.ShapeDtypeStruct((TILE, TILE), jnp.f...  4.56 us
  transfers between devices with their start and end apart: 6, of which 2 were waited for; matrix products, arithmetic and copies ran while one was open for 0% of the time, Pallas kernels for 5%

profile of v8, /device:TPU:1, one launch (start us, length us, event | category | flops | bytes accessed | tf_op | source)
XLA Modules:
  0.0 121.2 jit_solution(12412565211842181679)
XLA Ops:
  0.6 2.2 %pack_tiles.1 = (bf16[2320,128]{1,0:T(8,128)(2,1)}, bf16[2320,128]{1,0:T(8,128)(2,1)}) custom-call(s32[1,18]{1,0:T(1,128)} %left_slots.1, s32[1,18]{1,0:T(1,128)} %right_slots.1, bf16[2304,128]{1,0:T(8,128)(2,1)} %bitcast.10, bf16[2304,128]{1,0:T(8,128)(2,1)} %bitcast.11), custom_call_target="tpu_custom_call" | custom-call | tf_op jit(solution)/shard_map/pack_tiles/pallas_call | solution.py:62
  2.8 7.6 %collective-permute-start.1 = (bf16[2320,128]{1,0:T(8,128)(2,1)}, bf16[2320,128]{1,0:T(8,128)(2,1)}, u32[]{:S(2)}, u32[]{:S(2)}) collective-permute-start(bf16[2320,128]{1,0:T(8,128)(2,1)} %get-tuple-element.12.left_0), channel_id=1, source_target_pairs={{0,31},{1,0},{2,1},{3,2},{4,3},{5,4},{6,5},{7,6},{8,7},{9,8},{10,9... | collective-permute-start | bytes 1781768 | tf_op jit(solution)/shard_map/ppermute | solution.py:224
  10.4 8.5 %collective-permute-start.2 = (bf16[2320,128]{1,0:T(8,128)(2,1)}, bf16[2320,128]{1,0:T(8,128)(2,1)S(1)}, u32[]{:S(2)}, u32[]{:S(2)}) collective-permute-start(bf16[2320,128]{1,0:T(8,128)(2,1)} %get-tuple-element.11.right_0), channel_id=1, source_target_pairs={{0,928},{1,929},{2,930},{3,931},{4,932},{5,933},{6,934},{7,935},{8... | collective-permute-start | bytes 1781768 | tf_op jit(solution)/shard_map/ppermute | solution.py:224
  18.9 11.9 %collective-permute-start = (bf16[2320,128]{1,0:T(8,128)(2,1)}, bf16[2320,128]{1,0:T(8,128)(2,1)S(1)}, u32[]{:S(2)}, u32[]{:S(2)}) collective-permute-start(bf16[2320,128]{1,0:T(8,128)(2,1)} %get-tuple-element.11.right_0), channel_id=1, source_target_pairs={{0,960},{1,961},{2,962},{3,963},{4,964},{5,965},{6,966},{7,967},{8... | collective-permute-start | bytes 1781768 | tf_op jit(solution)/shard_map/ppermute | solution.py:224
  30.8 3.6 %collective-permute-start.4 = (bf16[2320,128]{1,0:T(8,128)(2,1)}, bf16[2320,128]{1,0:T(8,128)(2,1)}, u32[]{:S(2)}, u32[]{:S(2)}) collective-permute-start(bf16[2320,128]{1,0:T(8,128)(2,1)} %get-tuple-element.12.left_0), channel_id=1, source_target_pairs={{0,29},{1,30},{2,31},{3,0},{4,1},{5,2},{6,3},{7,4},{8,5},{9,6},{10... | collective-permute-start | bytes 1781768 | tf_op jit(solution)/shard_map/ppermute | solution.py:224
  34.4 0.0 collective-permute-done.1.left_1
  34.4 2.6 %collective-permute-start.3 = (bf16[2320,128]{1,0:T(8,128)(2,1)}, bf16[2320,128]{1,0:T(8,128)(2,1)S(1)}, u32[]{:S(2)}, u32[]{:S(2)}) collective-permute-start(bf16[2320,128]{1,0:T(8,128)(2,1)} %collective-permute-done.1.left_1), channel_id=1, source_target_pairs={{0,31},{1,0},{2,1},{3,2},{4,3},{5,4},{6,5},{7,6},{8,7},{9,8},{10,9... | collective-permute-start | bytes 1781768 | tf_op jit(solution)/shard_map/ppermute | solution.py:224
  37.0 0.0 collective-permute-done.2.right_1
  37.0 0.0 copy-start
  37.0 1.1 copy-done
  38.1 0.0 copy-start.1
  38.1 1.1 copy-done.1
  39.2 4.6 %first_products.1.accum = f32[768,768]{1,0:T(8,128)S(1)} custom-call(bf16[2320,128]{1,0:T(8,128)(2,1)S(1)} %copy-done, bf16[2320,128]{1,0:T(8,128)(2,1)S(1)} %copy-done.1, bf16[2320,128]{1,0:T(8,128)(2,1)} %collective-permute-done.1.left_1, bf16[2320,128]{1,0:T(8,128)(2,1)S(1)} %collective-permute-done.2.right_1), custom_call_target="tpu_custom_call" | custom-call | flops 1000 | bytes 1000 | tf_op jit(solution)/shard_map/first_products/pallas_call | solution.py:174
  43.7 26.1 %collective-permute-done.right_2 = bf16[2320,128]{1,0:T(8,128)(2,1)S(1)} collective-permute-done((bf16[2320,128]{1,0:T(8,128)(2,1)}, bf16[2320,128]{1,0:T(8,128)(2,1)S(1)}, u32[]{:S(2)}, u32[]{:S(2)}) %collective-permute-start) | collective-permute-done | bytes 593952 | tf_op jit(solution)/shard_map/ppermute | solution.py:224
  69.9 2.4 %collective-permute-start.5 = (bf16[2320,128]{1,0:T(8,128)(2,1)S(1)}, bf16[2320,128]{1,0:T(8,128)(2,1)}, u32[]{:S(2)}, u32[]{:S(2)}) collective-permute-start(bf16[2320,128]{1,0:T(8,128)(2,1)S(1)} %collective-permute-done.right_2), channel_id=1, source_target_pairs={{0,32},{1,33},{2,34},{3,35},{4,36},{5,37},{6,38},{7,39},{8,40},{9,... | collective-permute-start | bytes 1781768 | tf_op jit(solution)/shard_map/ppermute | solution.py:224
  72.3 0.0 collective-permute-done.3.left_2
  72.3 1.1 place_forwarded.1
  73.4 0.0 collective-permute-done.4.left_3
  73.4 0.6 collective-permute-done.5.right_3
  74.0 5.3 %last_product.1 = (bf16[768,768]{1,0:T(8,128)(2,1)}, f32[32,128]{1,0:T(8,128)S(1)}) custom-call(s32[1]{0:T(128)} %bitcast.on_diagonal, f32[768,768]{1,0:T(8,128)S(1)} %first_products.1.accum, bf16[896,768]{1,0:T(8,128)(2,1)S(1)} %get-tuple-element.15.left_early, bf16[896,768]{1,0:T(8,128)(2,1)S(1)} %get-tuple-element.16.right_early, ...), custom_call_target="tpu_custom_call" | custom-call | flops 1000 | bytes 1000 | tf_op jit(solution)/shard_map/last_product/pallas_call | solution.py:203
  79.4 19.9 %all_to_all.15 = f32[32,1,128]{2,1,0:T(1,128)S(1)} all-to-all(f32[32,1,128]{2,1,0:T(1,128)S(1)} %bitcast.9), channel_id=1, replica_groups=mesh['row'=32,'col'=32] {'row'}, dimensions={0} | all-to-all | bytes 32768 | tf_op jit(solution)/shard_map/all_to_all | solution.py:228
  99.3 0.1 reduce_sum.18
  99.3 17.7 %all_to_all.16 = f32[32,1,128]{2,1,0:T(1,128)S(1)} all-to-all(f32[32,1,128]{2,1,0:T(1,128)S(1)} %broadcast_in_dim.2), channel_id=1, replica_groups=mesh['row'=32,'col'=32] {'col'}, dimensions={0} | all-to-all | bytes 32768 | tf_op jit(solution)/shard_map/all_to_all | solution.py:228
  117.1 0.6 fusion
  (2 shorter events, 0.0 us)
Async XLA Ops:
  2.8 31.6 %collective-permute-start.1 = (bf16[2320,128]{1,0:T(8,128)(2,1)}, bf16[2320,128]{1,0:T(8,128)(2,1)}, u32[]{:S(2)}, u32[]{:S(2)}) collective-permute-start(bf16[2320,128]{1,0:T(8,128)(2,1)} %get-tuple-element.12.left_0), channel_id=1, source_target_pairs={{0,31},{1,0},{2,1},{3,2},{4,3},{5,4},{6,5},{7,6},{8,7},{9,8},{10,9... | collective-permute-start | bytes 1781768 | tf_op jit(solution)/shard_map/ppermute | solution.py:224
  10.4 26.6 %collective-permute-start.2 = (bf16[2320,128]{1,0:T(8,128)(2,1)}, bf16[2320,128]{1,0:T(8,128)(2,1)S(1)}, u32[]{:S(2)}, u32[]{:S(2)}) collective-permute-start(bf16[2320,128]{1,0:T(8,128)(2,1)} %get-tuple-element.11.right_0), channel_id=1, source_target_pairs={{0,928},{1,929},{2,930},{3,931},{4,932},{5,933},{6,934},{7,935},{8... | collective-permute-start | bytes 1781768 | tf_op jit(solution)/shard_map/ppermute | solution.py:224
  18.9 51.0 %collective-permute-start = (bf16[2320,128]{1,0:T(8,128)(2,1)}, bf16[2320,128]{1,0:T(8,128)(2,1)S(1)}, u32[]{:S(2)}, u32[]{:S(2)}) collective-permute-start(bf16[2320,128]{1,0:T(8,128)(2,1)} %get-tuple-element.11.right_0), channel_id=1, source_target_pairs={{0,960},{1,961},{2,962},{3,963},{4,964},{5,965},{6,966},{7,967},{8... | collective-permute-start | bytes 1781768 | tf_op jit(solution)/shard_map/ppermute | solution.py:224
  30.8 42.6 %collective-permute-start.4 = (bf16[2320,128]{1,0:T(8,128)(2,1)}, bf16[2320,128]{1,0:T(8,128)(2,1)}, u32[]{:S(2)}, u32[]{:S(2)}) collective-permute-start(bf16[2320,128]{1,0:T(8,128)(2,1)} %get-tuple-element.12.left_0), channel_id=1, source_target_pairs={{0,29},{1,30},{2,31},{3,0},{4,1},{5,2},{6,3},{7,4},{8,5},{9,6},{10... | collective-permute-start | bytes 1781768 | tf_op jit(solution)/shard_map/ppermute | solution.py:224
  34.4 37.9 %collective-permute-start.3 = (bf16[2320,128]{1,0:T(8,128)(2,1)}, bf16[2320,128]{1,0:T(8,128)(2,1)S(1)}, u32[]{:S(2)}, u32[]{:S(2)}) collective-permute-start(bf16[2320,128]{1,0:T(8,128)(2,1)} %collective-permute-done.1.left_1), channel_id=1, source_target_pairs={{0,31},{1,0},{2,1},{3,2},{4,3},{5,4},{6,5},{7,6},{8,7},{9,8},{10,9... | collective-permute-start | bytes 1781768 | tf_op jit(solution)/shard_map/ppermute | solution.py:224
  37.0 1.1 copy-start
  38.1 1.1 copy-start.1
  69.9 4.1 %collective-permute-start.5 = (bf16[2320,128]{1,0:T(8,128)(2,1)S(1)}, bf16[2320,128]{1,0:T(8,128)(2,1)}, u32[]{:S(2)}, u32[]{:S(2)}) collective-permute-start(bf16[2320,128]{1,0:T(8,128)(2,1)S(1)} %collective-permute-done.right_2), channel_id=1, source_target_pairs={{0,32},{1,33},{2,34},{3,35},{4,36},{5,37},{6,38},{7,39},{8,40},{9,... | collective-permute-start | bytes 1781768 | tf_op jit(solution)/shard_map/ppermute | solution.py:224
